TPU v7x, 512 devices: a whole 4x4x16 slice. The times are simulated.
512 devices in a mesh: leaf: 32 (over x, y, core), front: 16 (over z).
Axes of the slice: x: 4, y: 4, z: 16, core: 2. Of those that a mesh axis runs over, the one named last changes fastest.
Arguments:
- panel_0: float32 [2, 1024, 1024], P(None, 'front', 'leaf'), as said below
- panel_1: float32 [2, 1024, 2048], P(None, 'front', 'leaf'), as said below
- panel_2: float32 [2, 1024, 4096], P(None, 'front', 'leaf'), as said below
- panel_3: float32 [2, 1024, 8192], P(None, 'front', 'leaf'), as said below
- load_0: float32 [1024, 128], P('leaf'), may hold values from -6 to 6
- load_1: float32 [2048, 128], P('leaf'), may hold values from -6 to 6
- load_2: float32 [4096, 128], P('leaf'), may hold values from -6 to 6
- load_3: float32 [8192, 128], P('leaf'), may hold values from -6 to 6
- inflow: float32 [8, 1024, 128], P(None, 'front'), may hold values from -6 to 6
- above_solution: float32 [1024, 128], replicated, may hold values from -6 to 6
- block_maps: int32 [14, 16], replicated, may hold values from 0 to 31, as said below
Outputs:
- solution_0: float32 [1024, 128], P(('leaf', 'front'))
- solution_1: float32 [2048, 128], P(('leaf', 'front'))
- solution_2: float32 [4096, 128], P(('leaf', 'front'))
- solution_3: float32 [8192, 128], P(('leaf', 'front'))
- top_update: float32 [1024, 128], P('front')
Inputs may be any that keep to these rules, and one draw needn't show every extreme that they name: `block_maps`: the 16 entries of each row are distinct. `panel_0`: within each front the pivot block K is lower triangular with diagonal entries of 0.8 to 1.25. `panel_1`: within each front the pivot block K is lower triangular with diagonal entries of 0.8 to 1.25. `panel_2`: within each front the pivot block K is lower triangular with diagonal entries of 0.8 to 1.25. `panel_3`: within each front the pivot block K is lower triangular with diagonal entries of 0.8 to 1.25.
All inputs are finite; a program needn't handle non-finite values.
Results may differ from a plain program's by a relative error of at most 0.00013.
Values sent between devices are 32-bit elements; how exact they have to be, the bound alone decides.
No kernel may reach another device: no remote copies, remote signals or barrier semaphores. Data moves between devices by JAX's collectives and lax.ppermute only.
A program may use at most 64 MiB of HBM per device.

v0:
```python
import jax
import jax.numpy as jnp
from jax import lax
from jax.sharding import PartitionSpec as P

exact_precision = lax.Precision.HIGHEST


def partner_2(value, axis, distance):
    mask = 2**distance
    pairs = [(source, source ^ mask) for source in range(lax.axis_size(axis))]
    return lax.ppermute(value, axis, pairs)


def group_total(partial_sum, group_bits, level_id):
    leaf_pos = lax.axis_index("leaf")
    group_count = 1 << level_id
    slot_id = leaf_pos >> group_bits
    chosen = (jnp.arange(group_count, dtype=jnp.int32) == slot_id).astype(jnp.float32)
    spread_out = chosen.reshape((group_count,) + (1,) * partial_sum.ndim) * partial_sum[None]
    totals = lax.psum(spread_out, "leaf")
    return lax.dynamic_index_in_dim(totals, slot_id, 0, keepdims=False)


def group_concat(column_block, group_bits):
    leaf_pos = lax.axis_index("leaf")
    for section_bit in range(group_bits):
        partner = partner_2(column_block, "leaf", section_bit)
        upper_half = leaf_pos >> section_bit & 1 == 1
        column_block = jnp.where(
            upper_half,
            jnp.concatenate([partner, column_block], 0),
            jnp.concatenate([column_block, partner], 0),
        )
    return column_block


def place_blocks(map_row, values, block_rows):
    block_count = map_row.shape[0]
    targets = jnp.arange(2 * block_count, dtype=jnp.int32)
    selector_matrix = (targets[:, None] == map_row[None, :]).astype(jnp.float32)
    factor_blocks = values.reshape(block_count, block_rows, values.shape[1])
    return jnp.einsum("du,uye->dye", selector_matrix, factor_blocks, precision=exact_precision)


def lift_update(update_block, level_id, group_bits, block_maps, sep_rows):
    leaf_pos = lax.axis_index("leaf")
    front_pos = lax.axis_index("front")
    block_rows = update_block.shape[0]
    block_count = sep_rows // block_rows
    group_size = 1 << group_bits
    child_id = leaf_pos >> group_bits
    base_row = (1 << level_id) - 2
    own_map = lax.dynamic_index_in_dim(block_maps, base_row + child_id, 0, keepdims=False)
    parent_pos = leaf_pos % (2 * group_size)
    parent_rows = sep_rows // (2 * group_size)
    other_map = lax.dynamic_index_in_dim(block_maps, base_row + (child_id ^ 1), 0, keepdims=False)
    partner_block = partner_2(update_block, "leaf", group_bits)
    own_full, other_full = (
        lax.all_gather(update_block, "front", axis=0, tiled=True),
        lax.all_gather(partner_block, "front", axis=0, tiled=True),
    )
    placed = place_blocks(own_map, own_full, block_rows) + place_blocks(
        other_map, other_full, block_rows
    )
    separator = placed[:block_count].reshape(sep_rows, -1)
    sep_part = lax.dynamic_slice_in_dim(separator, parent_pos * parent_rows, parent_rows, 0)
    border = lax.dynamic_index_in_dim(placed, block_count + front_pos, 0, keepdims=False)
    return (sep_part, border)


def on_device(
    panel_0,
    panel_1,
    panel_2,
    panel_3,
    load_0,
    load_1,
    load_2,
    load_3,
    inflow,
    above_solution,
    block_maps,
):
    panels = (panel_0, panel_1, panel_2, panel_3)
    load_list = (load_0, load_1, load_2, load_3)
    level_count = len(panels)
    leaf_pos = lax.axis_index("leaf")
    front_pos = lax.axis_index("front")
    front_count = lax.axis_size("front")
    total_bits = lax.axis_size("leaf").bit_length() - 1
    block_rows = panel_0.shape[1]
    sep_rows = block_rows * front_count
    solved = [None] * level_count
    lifted = None
    top_block = None
    for level_id in range(level_count - 1, -1, -1):
        group_bits = total_bits - level_id
        right_side = load_list[level_id]
        if level_id == level_count - 1:
            front_id = leaf_pos >> group_bits
            border = lax.dynamic_index_in_dim(inflow, front_id, 0, keepdims=False)
        else:
            right_side = right_side + lifted[0]
            border = lifted[1]
        partial_sum = jnp.einsum(
            "ksc,cr->ksr", panels[level_id], right_side, precision=exact_precision
        )
        totals = group_total(partial_sum, group_bits, level_id)
        solved[level_id] = totals[0]
        update_block = border - totals[1]
        if level_id > 0:
            lifted = lift_update(update_block, level_id, group_bits, block_maps, sep_rows)
        else:
            top_block = update_block
    upper_full = above_solution
    upper_block = lax.dynamic_slice_in_dim(above_solution, front_pos * block_rows, block_rows, 0)
    targets = jnp.arange(2 * front_count, dtype=jnp.int32)
    pieces = []
    for level_id in range(level_count):
        group_bits = total_bits - level_id
        stacked = jnp.stack([solved[level_id], -upper_block])
        partial_sum = jnp.einsum(
            "ksc,ksr->cr", panels[level_id], stacked, precision=exact_precision
        )
        column_block = lax.psum(partial_sum, "front")
        span_rows = column_block.shape[0] // front_count
        pieces.append(lax.dynamic_slice_in_dim(column_block, front_pos * span_rows, span_rows, 0))
        if level_id < level_count - 1:
            full_solution = group_concat(column_block, group_bits)
            ancestor_blocks = jnp.concatenate([full_solution, upper_full], 0).reshape(
                2 * front_count, block_rows, -1
            )
            child_id = leaf_pos >> group_bits - 1
            child_map = lax.dynamic_index_in_dim(
                block_maps, (2 << level_id) - 2 + child_id, 0, keepdims=False
            )
            selector_matrix = (child_map[:, None] == targets[None, :]).astype(jnp.float32)
            upper_factor_blocks = jnp.einsum(
                "gq,qzk->gzk", selector_matrix, ancestor_blocks, precision=exact_precision
            )
            upper_full = upper_factor_blocks.reshape(sep_rows, -1)
            upper_block = lax.dynamic_index_in_dim(
                upper_factor_blocks, front_pos, 0, keepdims=False
            )
    return (pieces[0], pieces[1], pieces[2], pieces[3], top_block)


def solution(mesh):
    in_specs = (
        P(None, "front", "leaf"),
        P(None, "front", "leaf"),
        P(None, "front", "leaf"),
        P(None, "front", "leaf"),
        P("leaf", None),
        P("leaf", None),
        P("leaf", None),
        P("leaf", None),
        P(None, "front", None),
        P(),
        P(),
    )
    out_specs = (
        P(("leaf", "front"), None),
        P(("leaf", "front"), None),
        P(("leaf", "front"), None),
        P(("leaf", "front"), None),
        P("front", None),
    )
    return jax.shard_map(
        on_device, mesh=mesh, in_specs=in_specs, out_specs=out_specs, check_vma=False
    )
```

profile of v0, /device:TPU:1, one launch (start us, length us, event | category | flops | bytes accessed | tf_op | source)
XLA Modules:
  0.0 1200.6 jit_solution(1407500976551751530)
XLA Ops:
  11.2 139.5 %all-reduce.7.cloned.1.call-done = f32[8,2,64,128]{3,2,1,0:T(8,128)} async-done(((f32[8,2,64,128]{3,2,1,0:T(8,128)}), f32[8,2,64,128]{3,2,1,0:T(8,128)}) %all-reduce.7.cloned.1.call-update) | async-done | bytes 524304 | tf_op jit(solution)/shard_map/psum | solution.py:21
  151.5 4.1 collective-permute-start
  155.6 27.0 %all_gather.18 = f32[1024,128]{1,0:T(8,128)S(1)} all-gather(f32[64,128]{1,0:T(8,128)S(1)} %fusion.32), channel_id=1, replica_groups=mesh['leaf'=32,'front'=16] {'front'}, dimensions={0}, use_global_device_ids=true | all-gather | bytes 557056 | tf_op jit(solution)/shard_map/all_gather | solution.py:60
  183.5 22.7 %all_gather.19 = f32[1024,128]{1,0:T(8,128)S(1)} all-gather(f32[64,128]{1,0:T(8,128)S(1)} %collective-permute-done), channel_id=1, replica_groups=mesh['leaf'=32,'front'=16] {'front'}, dimensions={0}, use_global_device_ids=true | all-gather | bytes 557056 | tf_op jit(solution)/shard_map/all_gather | solution.py:61
  209.3 142.0 %all-reduce.9.cloned.1.call-done = f32[4,2,64,128]{3,2,1,0:T(8,128)} async-done(((f32[4,2,64,128]{3,2,1,0:T(8,128)}), f32[4,2,64,128]{3,2,1,0:T(8,128)}) %all-reduce.9.cloned.1.call-update) | async-done | bytes 262160 | tf_op jit(solution)/shard_map/psum | solution.py:21
  352.1 2.9 collective-permute-start.1
  355.0 26.6 %all_gather.20 = f32[1024,128]{1,0:T(8,128)S(1)} all-gather(f32[64,128]{1,0:T(8,128)S(1)} %fusion.31), channel_id=1, replica_groups=mesh['leaf'=32,'front'=16] {'front'}, dimensions={0}, use_global_device_ids=true | all-gather | bytes 557056 | tf_op jit(solution)/shard_map/all_gather | solution.py:60
  382.6 23.0 %all_gather.21 = f32[1024,128]{1,0:T(8,128)S(1)} all-gather(f32[64,128]{1,0:T(8,128)S(1)} %collective-permute-done.1), channel_id=1, replica_groups=mesh['leaf'=32,'front'=16] {'front'}, dimensions={0}, use_global_device_ids=true | all-gather | bytes 557056 | tf_op jit(solution)/shard_map/all_gather | solution.py:61
  408.5 140.2 %all-reduce.11.cloned.1.call-done = f32[2,2,64,128]{3,2,1,0:T(8,128)} async-done(((f32[2,2,64,128]{3,2,1,0:T(8,128)}), f32[2,2,64,128]{3,2,1,0:T(8,128)}) %all-reduce.11.cloned.1.call-update) | async-done | bytes 131088 | tf_op jit(solution)/shard_map/psum | solution.py:21
  549.5 4.0 collective-permute-start.2
  553.5 26.2 %all_gather.22 = f32[1024,128]{1,0:T(8,128)S(1)} all-gather(f32[64,128]{1,0:T(8,128)S(1)} %fusion.30), channel_id=1, replica_groups=mesh['leaf'=32,'front'=16] {'front'}, dimensions={0}, use_global_device_ids=true | all-gather | bytes 557056 | tf_op jit(solution)/shard_map/all_gather | solution.py:60
  580.6 24.0 %all_gather.23 = f32[1024,128]{1,0:T(8,128)S(1)} all-gather(f32[64,128]{1,0:T(8,128)S(1)} %collective-permute-done.2), channel_id=1, replica_groups=mesh['leaf'=32,'front'=16] {'front'}, dimensions={0}, use_global_device_ids=true | all-gather | bytes 557056 | tf_op jit(solution)/shard_map/all_gather | solution.py:61
  607.4 136.1 %all-reduce.13.cloned.1.call-done = f32[1,2,64,128]{3,2,1,0:T(8,128)} async-done(((f32[1,2,64,128]{3,2,1,0:T(8,128)}), f32[1,2,64,128]{3,2,1,0:T(8,128)}) %all-reduce.13.cloned.1.call-update) | async-done | bytes 65552 | tf_op jit(solution)/shard_map/psum | solution.py:21
  744.5 43.6 %psum.60 = f32[32,128]{1,0:T(8,128)S(1)} all-reduce(f32[32,128]{1,0:T(8,128)S(1)} %convolution_bitcast_fusion.5), channel_id=1, replica_groups=mesh['leaf'=32,'front'=16] {'front'}, use_global_device_ids=true, to_apply=%region_4.5 | all-reduce | flops 4096 | bytes 32768 | tf_op jit(solution)/shard_map/psum | solution.py:126
  788.1 15.6 %collective-permute-start.3 = (f32[32,128]{1,0:T(8,128)S(1)}, f32[32,128]{1,0:T(8,128)S(1)}, u32[]{:S(2)}, u32[]{:S(2)}) collective-permute-start(f32[32,128]{1,0:T(8,128)S(1)} %psum.60), channel_id=1, source_target_pairs={{0,16},{16,0},{32,48},{48,32},{64,80},{80,64},{96,112},{112,96},{1... | collective-permute-start | bytes 49160 | tf_op jit(solution)/shard_map/ppermute | solution.py:12
  809.1 3.6 collective-permute-start.5
  812.7 2.9 collective-permute-done.5
  817.9 3.5 collective-permute-done.6
  821.4 3.6 collective-permute-start.7
  825.7 4.3 collective-permute-done.7
  831.6 39.5 %psum.61 = f32[64,128]{1,0:T(8,128)S(1)} all-reduce(f32[64,128]{1,0:T(8,128)S(1)} %convolution_bitcast_fusion.4), channel_id=1, replica_groups=mesh['leaf'=32,'front'=16] {'front'}, use_global_device_ids=true, to_apply=%region_5.6 | all-reduce | flops 8192 | bytes 65536 | tf_op jit(solution)/shard_map/psum | solution.py:126
  871.1 20.8 %collective-permute-start.8 = (f32[64,128]{1,0:T(8,128)S(1)}, f32[64,128]{1,0:T(8,128)S(1)}, u32[]{:S(2)}, u32[]{:S(2)}) collective-permute-start(f32[64,128]{1,0:T(8,128)S(1)} %psum.61), channel_id=1, source_target_pairs={{0,16},{16,0},{32,48},{48,32},{64,80},{80,64},{96,112},{112,96},{1... | collective-permute-start | bytes 98312 | tf_op jit(solution)/shard_map/ppermute | solution.py:12
  895.0 2.8 collective-permute-done.9
  897.8 3.6 collective-permute-start.10
  901.4 3.6 collective-permute-done.10
  908.4 3.8 collective-permute-done.11
  914.5 120.2 %all-reduce.15.cloned.1.call-done = f32[128,128]{0,1:T(8,128)} async-done(((f32[128,128]{0,1:T(8,128)}), f32[128,128]{0,1:T(8,128)}) %all-reduce.15.cloned.1.call-update) | async-done | bytes 65552 | tf_op jit(solution)/shard_map/psum | solution.py:126
  1034.7 13.6 %collective-permute-start.12 = (f32[128,128]{0,1:T(8,128)}, f32[128,128]{0,1:T(8,128)S(1)}, u32[]{:S(2)}, u32[]{:S(2)}) collective-permute-start(f32[128,128]{0,1:T(8,128)} %all-reduce.15.cloned.1.call-done), channel_id=1, source_target_pairs={{0,16},{16,0},{32,48},{48,32},{64,80},{80,64},{96,112},{112,96},{1... | collective-permute-start | bytes 196616 | tf_op jit(solution)/shard_map/ppermute | solution.py:12
  1050.3 3.1 collective-permute-start.13
  1057.0 4.6 collective-permute-start.14
  1063.2 3.8 collective-permute-done.14
  1071.2 121.0 %all-reduce.17.cloned.1.call-done = f32[256,128]{0,1:T(8,128)} async-done(((f32[256,128]{0,1:T(8,128)}), f32[256,128]{0,1:T(8,128)}) %all-reduce.17.cloned.1.call-update) | async-done | bytes 131088 | tf_op jit(solution)/shard_map/psum | solution.py:126
  (117 shorter events, 49.9 us)
Async XLA Ops:
  7.2 0.9 copy-start
  7.2 143.6 %all-reduce.7.cloned.1.call-start = ((), (), s32[]{:S(2)}) async-start(), calls=%async_computation | async-start | bytes 1048576 | tf_op jit(solution)/shard_map/psum | solution.py:21
  10.2 341.2 %all-reduce.9.cloned.1.call-start = ((), (), s32[]{:S(2)}) async-start(), calls=%async_computation.1 | async-start | bytes 524288 | tf_op jit(solution)/shard_map/psum | solution.py:21
  151.5 32.0 %collective-permute-start = (f32[64,128]{1,0:T(8,128)S(1)}, f32[64,128]{1,0:T(8,128)S(1)}, u32[]{:S(2)}, u32[]{:S(2)}) collective-permute-start(f32[64,128]{1,0:T(8,128)S(1)} %fusion.32), channel_id=1, source_target_pairs={{0,64},{16,80},{32,96},{48,112},{64,0},{80,16},{96,32},{112,48},{1... | collective-permute-start | bytes 98312 | tf_op jit(solution)/shard_map/ppermute | solution.py:12
  207.3 0.8 copy-start.3
  207.3 0.9 copy-start.7
  209.2 339.5 %all-reduce.11.cloned.1.call-start = ((), (), s32[]{:S(2)}) async-start(), calls=%async_computation.2 | async-start | bytes 262144 | tf_op jit(solution)/shard_map/psum | solution.py:21
  352.1 30.5 %collective-permute-start.1 = (f32[64,128]{1,0:T(8,128)S(1)}, f32[64,128]{1,0:T(8,128)S(1)}, u32[]{:S(2)}, u32[]{:S(2)}) collective-permute-start(f32[64,128]{1,0:T(8,128)S(1)} %fusion.31), channel_id=1, source_target_pairs={{0,128},{16,144},{32,160},{48,176},{64,192},{80,208},{96,224},{112... | collective-permute-start | bytes 98312 | tf_op jit(solution)/shard_map/ppermute | solution.py:12
  406.6 0.8 copy-start.2
  406.6 0.8 copy-start.8
  408.4 335.1 %all-reduce.13.cloned.1.call-start = ((), (), s32[]{:S(2)}) async-start(), calls=%async_computation.3 | async-start | bytes 131072 | tf_op jit(solution)/shard_map/psum | solution.py:21
  549.5 31.1 %collective-permute-start.2 = (f32[64,128]{1,0:T(8,128)S(1)}, f32[64,128]{1,0:T(8,128)S(1)}, u32[]{:S(2)}, u32[]{:S(2)}) collective-permute-start(f32[64,128]{1,0:T(8,128)S(1)} %fusion.30), channel_id=1, source_target_pairs={{0,256},{16,272},{32,288},{48,304},{64,320},{80,336},{96,352},{112... | collective-permute-start | bytes 98312 | tf_op jit(solution)/shard_map/ppermute | solution.py:12
  605.6 0.8 copy-start.5
  605.6 0.8 copy-start.9
  605.6 1.7 copy-start.1
  607.3 427.4 %all-reduce.15.cloned.1.call-start = ((), (), s32[]{:S(2)}) async-start(), calls=%async_computation.4 | async-start | bytes 131072 | tf_op jit(solution)/shard_map/psum | solution.py:126
  788.1 16.4 %collective-permute-start.3 = (f32[32,128]{1,0:T(8,128)S(1)}, f32[32,128]{1,0:T(8,128)S(1)}, u32[]{:S(2)}, u32[]{:S(2)}) collective-permute-start(f32[32,128]{1,0:T(8,128)S(1)} %psum.60), channel_id=1, source_target_pairs={{0,16},{16,0},{32,48},{48,32},{64,80},{80,64},{96,112},{112,96},{1... | collective-permute-start | bytes 49160 | tf_op jit(solution)/shard_map/ppermute | solution.py:12
  804.5 4.6 collective-permute-start.4
  809.1 6.5 collective-permute-start.5
  815.7 5.7 collective-permute-start.6
  821.4 8.6 collective-permute-start.7
  871.1 21.7 %collective-permute-start.8 = (f32[64,128]{1,0:T(8,128)S(1)}, f32[64,128]{1,0:T(8,128)S(1)}, u32[]{:S(2)}, u32[]{:S(2)}) collective-permute-start(f32[64,128]{1,0:T(8,128)S(1)} %psum.61), channel_id=1, source_target_pairs={{0,16},{16,0},{32,48},{48,32},{64,80},{80,64},{96,112},{112,96},{1... | collective-permute-start | bytes 98312 | tf_op jit(solution)/shard_map/ppermute | solution.py:12
  892.8 5.0 collective-permute-start.9
  897.8 7.2 collective-permute-start.10
  905.1 7.1 collective-permute-start.11
  914.5 277.7 %all-reduce.17.cloned.1.call-start = ((), (), s32[]{:S(2)}) async-start(), calls=%async_computation.5 | async-start | bytes 262144 | tf_op jit(solution)/shard_map/psum | solution.py:126
  1034.7 14.7 %collective-permute-start.12 = (f32[128,128]{0,1:T(8,128)}, f32[128,128]{0,1:T(8,128)S(1)}, u32[]{:S(2)}, u32[]{:S(2)}) collective-permute-start(f32[128,128]{0,1:T(8,128)} %all-reduce.15.cloned.1.call-done), channel_id=1, source_target_pairs={{0,16},{16,0},{32,48},{48,32},{64,80},{80,64},{96,112},{112,96},{1... | collective-permute-start | bytes 196616 | tf_op jit(solution)/shard_map/ppermute | solution.py:12
  1050.3 6.6 collective-permute-start.13
  1054.3 7.9 copy-start.6
  1057.0 10.0 collective-permute-start.14
  1069.6 0.8 copy-start.4
Sparse Core Ops, SparseCore 0:
  11.2 139.5 all-reduce.6
  209.3 141.9 all-reduce.8
  408.5 140.1 all-reduce.10
  607.5 135.9 all-reduce.12
  914.6 120.0 all-reduce.14
  1069.7 122.4 all-reduce.16
where the time goes:
time: 1210 us; the launch traced here: 1200 us
  waiting for transfers between devices  832 us (69%)
  blocking collectives  233 us (19%)
  starting transfers between devices  88.7 us (7%)
  between operations  14.8 us (1%)
  matrix products  13.7 us (1%)
  local copies, waits for them, and re-layouts  12.1 us (1%)
    psum x4, waiting for transfers between devices, group_total(): totals = lax.psum(spread_out, 'leaf')  558 us
    psum x2, waiting for transfers between devices, on_device(): column_block = lax.psum(partial_sum, 'front')  241 us
    ppermute x15, starting transfers between devices, partner_2(): return lax.ppermute(value, axis, pairs)  88.4 us
    psum x2, blocking collectives, on_device(): column_block = lax.psum(partial_sum, 'front')  83.1 us
    all_gather x3, blocking collectives, lift_update(): lax.all_gather(update_block, 'front', axis=0, tiled=True)  79.8 us
    all_gather x3, blocking collectives, lift_update(): lax.all_gather(partner_block, 'front', axis=0, tiled=True)  69.7 us
    ppermute x15, waiting for transfers between devices, partner_2(): return lax.ppermute(value, axis, pairs)  32.6 us
  transfers between devices with their start and end apart: 21, of which 18 were waited for; matrix products, arithmetic and copies ran while one was open for 1% of the time, Pallas kernels for 0%

commit v1 on v0

v1 whole, which is shorter than its diff:
```python
import jax
import jax.numpy as jnp
from jax import lax
from jax.sharding import Mesh, PartitionSpec as P

exact = lax.Precision.HIGHEST
LEAF = ("xh", "xl", "y", "c")
SWAP = [(0, 1), (1, 0)]


def dot_nt(left, right):
    return lax.dot_general(left, right, (((1,), (1,)), ((), ())), precision=exact)


def dot_nn(left, right):
    return lax.dot_general(left, right, (((1,), (0,)), ((), ())), precision=exact)


def exchange(value, axes):
    return lax.all_to_all(value, axes, 0, 0)


def to_all(value, count):
    return jnp.broadcast_to(value[None], (count,) + value.shape)


def on_device(
    panel_0,
    panel_1,
    panel_2,
    panel_3,
    load_0,
    load_1,
    load_2,
    load_3,
    inflow,
    above_solution,
    block_maps,
):
    xh, xl = lax.axis_index("xh"), lax.axis_index("xl")
    y, c, z = lax.axis_index("y"), lax.axis_index("c"), lax.axis_index("z")
    x = 2 * xh + xl
    y_low = y & 1
    front_3 = 2 * x + (y >> 1)

    own_rows = jnp.concatenate(
        [panel_3[0], panel_3[1], panel_2[0], panel_1[0], panel_0[0], panel_0[1]], 1
    )
    gathered = lax.all_gather(own_rows, "z", axis=0, tiled=True)

    def pick_columns(value):
        return lax.dynamic_slice_in_dim(value, z * 8 + c * 4, 4, 1).T

    def pick_both(value):
        mine = lax.dynamic_slice_in_dim(value, z * 8, 8, 1).T
        return mine.reshape(2, 4, -1)

    loads = jnp.concatenate([pick_both(load_0), pick_both(load_1), pick_both(load_2)], 2)
    loads = exchange(loads, "c")
    load_0c = loads[:, :, :32].transpose(1, 0, 2).reshape(4, 64)
    load_1c = loads[:, :, 32:96].transpose(1, 0, 2).reshape(4, 128)
    load_2c = loads[:, :, 96:].transpose(1, 0, 2).reshape(4, 256)
    above = pick_columns(above_solution)

    part_3 = jnp.einsum("ksc,cr->rks", panel_3, load_3, precision=exact)
    border_3 = lax.dynamic_index_in_dim(inflow, front_3, 0, keepdims=False).T
    first = (y_low + c == 0).astype(jnp.float32)
    part_3 = jnp.concatenate([part_3[:, 0], first * border_3 - part_3[:, 1]], 1)
    couple = jnp.concatenate(
        [panel_2[1], jnp.concatenate([panel_1[1, :32], panel_1[1, 32:]], 1)], 0
    )
    payload = jnp.concatenate([part_3.reshape(16, 8, 128), to_all(couple, 16)], 1)
    got = exchange(payload, "z")
    vec = got[:, :8].reshape(16, 8, 2, 64).transpose(2, 1, 0, 3).reshape(2, 8, 1024)
    couple_2 = got[:, 8:72].reshape(1024, 128)
    couple_1 = got[:, 72:]
    couple_1 = jnp.stack([couple_1[..., :64], couple_1[..., 64:]], 1).reshape(1024, 64)

    couple_2o = lax.ppermute(couple_2, "c", SWAP)
    couple_1o = lax.ppermute(couple_1, "c", SWAP)

    def by_core(own, other):
        return jnp.where(c == 0, own, other), jnp.where(c == 0, other, own)

    def chip_nt(vector, own, other):
        width = own.shape[1]
        low, high = vector[:, :width], vector[:, width:]
        mine, rest = jnp.where(c == 0, low, high), jnp.where(c == 0, high, low)
        return dot_nt(mine, own) + dot_nt(rest, other)

    def chip_columns(keep, keep_o, take, take_o, y_vec, s_vec):
        own = dot_nn(y_vec, keep) - dot_nn(s_vec, take)
        other = dot_nn(y_vec, keep_o) - dot_nn(s_vec, take_o)
        low, high = by_core(own, other)
        return jnp.concatenate([low, high], 1)

    u_send = vec[1].reshape(2, 4, 1024)
    u_send = jnp.broadcast_to(u_send[None], (4, 2, 4, 1024))
    y_send = vec[0].reshape(2, 4, 2, 512).transpose(2, 0, 1, 3)
    y_send = jnp.broadcast_to(y_send[None], (2, 2, 2, 4, 512)).reshape(4, 2, 4, 512)
    got = exchange(jnp.concatenate([u_send, y_send], 3).reshape(8, 4, 1536), ("y", "c"))
    got = got.reshape(2, 4, 4, 1536).sum(1)
    update = got[..., :1024]
    y3_piece = lax.dynamic_index_in_dim(got[..., 1024:], y >> 1, 0, keepdims=False)

    def lifted(update, base, block, count):
        maps = lax.dynamic_slice_in_dim(block_maps, base, 2, 0).reshape(32)
        targets = block * count + jnp.arange(count, dtype=jnp.int32)
        targets = jnp.concatenate([targets, targets + 16])
        chosen = (maps[:, None] == targets[None, :]).astype(jnp.float32)
        blocks = update.reshape(2, 4, 16, 64).transpose(1, 0, 2, 3).reshape(4, 32, 64)
        placed = jnp.einsum("rnk,np->rpk", blocks, chosen, precision=exact)
        separator = placed[:, :count].reshape(4, count * 64)
        border = placed[:, count:].reshape(4, count * 64)
        whole = jnp.zeros((4, 1024), jnp.float32)
        border = lax.dynamic_update_slice_in_dim(whole, border, block * count * 64, 1)
        return separator, border

    separator, border = lifted(update, 6 + 2 * x, y, 4)
    b_2 = separator + load_2c
    update = border - chip_nt(b_2, couple_2, couple_2o)
    update = exchange(to_all(update, 8), ("xl", "y")).reshape(2, 4, 4, 1024).sum(1)

    separator, border = lifted(update, 2 + 2 * xh, 4 * xl + y, 2)
    b_1 = separator + load_1c
    update = border - chip_nt(b_1, couple_1, couple_1o)
    update = exchange(to_all(update, 16), ("xh", "xl", "y")).reshape(2, 8, 4, 1024).sum(1)

    top, rest = gathered[:, 640:], gathered[:, :640]
    top_o = lax.ppermute(top, "c", SWAP)
    rest_o = lax.ppermute(rest, "c", SWAP)
    pivot_1, pivot_1o = top[:, :64], top_o[:, :64]
    pivot_0, pivot_0o = top[:, 64:96], top_o[:, 64:96]
    couple_0, couple_0o = top[:, 96:], top_o[:, 96:]
    pivot_3, pivot_3o = rest[:, :256], rest_o[:, :256]
    couple_3, couple_3o = rest[:, 256:512], rest_o[:, 256:512]
    pivot_2, pivot_2o = rest[:, 512:], rest_o[:, 512:]
    separator, border = lifted(update, 0, 4 * x + y, 1)
    b_0 = separator + load_0c
    y0_part = chip_nt(b_0, pivot_0, pivot_0o)
    u0_part = border - chip_nt(b_0, couple_0, couple_0o)
    y1_part = chip_nt(b_1, pivot_1, pivot_1o)
    u0_send = u0_part.reshape(4, 16, 64).transpose(1, 0, 2)
    y1_send = y1_part.reshape(4, 8, 128).transpose(1, 0, 2)
    y1_send = jnp.concatenate([y1_send, y1_send], 0)
    payload = jnp.concatenate([to_all(y0_part, 16), y1_send, u0_send], 2)
    got = exchange(payload, ("xh", "xl", "y"))
    y_0 = got[..., :1024].sum(0)
    u0_piece = got[..., 1152:].sum(0)
    y1_piece = got[..., 1024:1152].reshape(2, 8, 4, 128).sum(1)
    y1_piece = lax.dynamic_index_in_dim(y1_piece, xh, 0, keepdims=False)

    def taken(row, x_vec, s_vec):
        chosen_map = lax.dynamic_index_in_dim(block_maps, row, 0, keepdims=False)
        targets = jnp.arange(32, dtype=jnp.int32)
        chosen = (targets[:, None] == chosen_map[None, :]).astype(jnp.float32)
        stacked = jnp.concatenate([x_vec, s_vec], 1).reshape(4, 32, 64)
        return jnp.einsum("rqk,qn->rnk", stacked, chosen, precision=exact).reshape(4, 1024)

    x0_piece = chip_columns(pivot_0, pivot_0o, couple_0, couple_0o, y_0, above)
    y2_part = chip_nt(b_2, pivot_2, pivot_2o)
    y2_send = y2_part.reshape(4, 4, 256).transpose(1, 0, 2)
    y2_send = to_all(y2_send, 4).reshape(16, 4, 256)
    same = jnp.concatenate([x0_piece, u0_piece, y1_piece], 1)
    payload = jnp.concatenate([to_all(same, 16), y2_send], 2)
    got = exchange(payload, ("xh", "xl", "y"))
    x_0 = got[..., :64].transpose(1, 0, 2).reshape(4, 1024)
    u_0 = got[..., 64:128].transpose(1, 0, 2).reshape(4, 1024)
    y_1 = got[..., 128:256].reshape(2, 8, 4, 128)
    y_1 = lax.dynamic_index_in_dim(y_1, xh, 0, keepdims=False)
    y_1 = y_1.transpose(1, 0, 2).reshape(4, 1024)
    y2_piece = lax.dynamic_index_in_dim(
        got[..., 256:].reshape(4, 4, 4, 256).sum(1), x, 0, keepdims=False
    )

    s_1 = taken(xh, x_0, above)
    x1_piece = chip_columns(pivot_1, pivot_1o, couple_1, couple_1o, y_1, s_1)
    got = exchange(to_all(jnp.concatenate([x1_piece, y2_piece], 1), 8), ("xl", "y"))
    x_1 = got[..., :128].transpose(1, 0, 2).reshape(4, 1024)
    y_2 = lax.dynamic_index_in_dim(got[..., 128:].reshape(2, 4, 4, 256), xl, 0, keepdims=False)
    y_2 = y_2.transpose(1, 0, 2).reshape(4, 1024)

    s_2 = taken(2 + x, x_1, s_1)
    x2_piece = chip_columns(pivot_2, pivot_2o, couple_2, couple_2o, y_2, s_2)
    got = exchange(to_all(jnp.concatenate([x2_piece, y3_piece], 1), 4), "y")
    x_2 = got[..., :256].transpose(1, 0, 2).reshape(4, 1024)
    y_3 = lax.dynamic_index_in_dim(got[..., 256:].reshape(2, 2, 4, 512), y >> 1, 0, keepdims=False)
    y_3 = y_3.transpose(1, 0, 2).reshape(4, 1024)

    s_3 = taken(6 + front_3, x_2, s_2)
    x3_piece = chip_columns(pivot_3, pivot_3o, couple_3, couple_3o, y_3, s_3)

    def to_rows(piece):
        return piece.reshape(4, 2, 16, -1).transpose(1, 2, 0, 3)

    u0_rows = jnp.broadcast_to(u_0.reshape(4, 16, 64).transpose(1, 0, 2)[None], (2, 16, 4, 64))
    payload = jnp.concatenate(
        [
            to_rows(x3_piece),
            to_rows(x2_piece),
            to_rows(x1_piece),
            to_rows(x0_piece),
            jnp.zeros((2, 16, 4, 34), jnp.float32),
            u0_rows,
        ],
        3,
    )
    got = exchange(payload.reshape(32, 4, 128), ("c", "z"))
    got = got.reshape(2, 16, 4, 128).transpose(3, 1, 0, 2).reshape(128, 128)
    return (got[28:30], got[24:28], got[16:24], got[:16], got[64:])


def solution(mesh):
    fine = Mesh(mesh.devices.reshape(2, 2, 4, 2, 16), ("xh", "xl", "y", "c", "z"))
    panel = P(None, "z", LEAF)
    load = P(LEAF, None)
    in_specs = (panel,) * 4 + (load,) * 4 + (P(None, "z", None), P(), P())
    out_specs = (P(LEAF + ("z",), None),) * 4 + (P("z", None),)
    return jax.shard_map(
        on_device, mesh=fine, in_specs=in_specs, out_specs=out_specs, check_vma=False
    )
```

time: 1210 us -> 260 us (0.21)
  waiting for transfers between devices: 832 us -> 70.9 us
  blocking collectives: 233 us -> 26.3 us
  matrix products: 13.7 us -> 33.3 us
  starting transfers between devices: 88.7 us -> 70.4 us
  local copies, waits for them, and re-layouts: 12.1 us -> 29.2 us
    psum x6 -> x0, waiting for transfers between devices: 799 us -> none  [the longest x4 558 us: group_total(): totals = lax.psum(spread_out, 'leaf')]
    all_gather x6 -> x0, blocking collectives: 150 us -> none  [the longest x3 79.8 us: lift_update(): lax.all_gather(update_block, 'front', axis=0, tiled=True)]
    psum x2 -> x0, blocking collectives: 83.1 us -> none  [on_device(): column_block = lax.psum(partial_sum, 'front')]
    ppermute x15 -> x4, starting transfers between devices: 88.4 us -> 14.7 us  [the longest x1 8.03 us: on_device(): rest_o = lax.ppermute(rest, 'c', SWAP)]
    all_to_all x0 -> x9, waiting for transfers between devices: none -> 69.5 us  [exchange(): return lax.all_to_all(value, axes, 0, 0)]
    all_to_all x0 -> x9, starting transfers between devices: none -> 55.6 us  [exchange(): return lax.all_to_all(value, axes, 0, 0)]
    ppermute x15 -> x4, waiting for transfers between devices: 32.6 us -> 1.39 us  [the longest x1 1.39 us: on_device(): top_o = lax.ppermute(top, 'c', SWAP)]
    all_to_all x0 -> x1, blocking collectives: none -> 26.3 us  [exchange(): return lax.all_to_all(value, axes, 0, 0)]
  transfers between devices with their start and end apart: 21 -> 14, of which waited for: 18 -> 9; matrix products, arithmetic and copies ran while one was open for 1% -> 15% of each run, Pallas kernels for 0% -> 0%
where the time goes in v1:
time: 260 us; the launch traced here: 258 us
  waiting for transfers between devices  70.9 us (27%)
  starting transfers between devices  70.4 us (27%)
  matrix products  33.3 us (13%)
  local copies, waits for them, and re-layouts  29.2 us (11%)
  blocking collectives  26.3 us (10%)
  between operations  14.8 us (6%)
  other arithmetic  12.7 us (5%)
    all_to_all x9, waiting for transfers between devices, exchange(): return lax.all_to_all(value, axes, 0, 0)  69.5 us
    all_to_all x9, starting transfers between devices, exchange(): return lax.all_to_all(value, axes, 0, 0)  55.6 us
    all_to_all x1, blocking collectives, exchange(): return lax.all_to_all(value, axes, 0, 0)  26.3 us
    dot_general x16, matrix products, dot_nn(): lax.dot_general(left, right, (((1,), (0,)), ((), ())), precision=exact)  18.4 us
    dot_general x12, matrix products, dot_nt(): lax.dot_general(left, right, (((1,), (1,)), ((), ())), precision=exact)  11.4 us
    ppermute x1, starting transfers between devices, on_device(): rest_o = lax.ppermute(rest, 'c', SWAP)  8.03 us
  transfers between devices with their start and end apart: 14, of which 9 were waited for; matrix products, arithmetic and copies ran while one was open for 15% of the time, Pallas kernels for 0%

profile of v1, /device:TPU:1, one launch (start us, length us, event | category | flops | bytes accessed | tf_op | source)
XLA Modules:
  0.0 257.6 jit_solution(2475632581650441713)
XLA Ops:
  10.7 10.1 %all-to-all-start.2 = ((f32[2,4,224]{2,1,0:T(4,128)}), f32[2,4,224]{2,1,0:T(4,128)S(1)}, u32[]{:S(2)}, u32[]{:S(2)}) async-start(f32[2,4,224]{2,1,0:T(4,128)} %pad_maximum_fusion.6), calls=%async_computation.2 | async-start | bytes 16384 | tf_op jit(solution)/shard_map/all_to_all | solution.py:20
  25.7 9.5 %all-to-all-start = ((f32[16,104,128]{2,1,0:T(8,128)}), f32[16,104,128]{2,1,0:T(8,128)S(1)}, u32[]{:S(2)}, u32[]{:S(2)}) async-start(f32[16,104,128]{2,1,0:T(8,128)} %pad_maximum_fusion), calls=%async_computation | async-start | bytes 1703936 | tf_op jit(solution)/shard_map/all_to_all | solution.py:20
  37.6 39.2 %all-to-all-done = f32[16,104,128]{2,1,0:T(8,128)S(1)} async-done(((f32[16,104,128]{2,1,0:T(8,128)}), f32[16,104,128]{2,1,0:T(8,128)S(1)}, u32[]{:S(2)}, u32[]{:S(2)}) %all-to-all-start) | async-done | bytes 852000 | tf_op jit(solution)/shard_map/all_to_all | solution.py:20
  77.9 9.7 %all-to-all-start.1 = ((f32[8,4,1536]{2,1,0:T(4,128)}), f32[8,4,1536]{2,1,0:T(4,128)S(1)}, u32[]{:S(2)}, u32[]{:S(2)}) async-start(f32[8,4,1536]{2,1,0:T(4,128)} %pad_maximum_fusion.3), calls=%async_computation.1 | async-start | bytes 393216 | tf_op jit(solution)/shard_map/all_to_all | solution.py:20
  87.7 1.9 collective-permute-start
  89.7 3.8 %all-to-all-done.1 = f32[8,4,1536]{2,1,0:T(4,128)S(1)} async-done(((f32[8,4,1536]{2,1,0:T(4,128)}), f32[8,4,1536]{2,1,0:T(4,128)S(1)}, u32[]{:S(2)}, u32[]{:S(2)}) %all-to-all-start.1) | async-done | bytes 196640 | tf_op jit(solution)/shard_map/all_to_all | solution.py:20
  95.9 4.0 %all-to-all-start.3 = ((f32[8,4,1024]{2,1,0:T(4,128)}), f32[8,4,1024]{2,1,0:T(4,128)}, u32[]{:S(2)}, u32[]{:S(2)}) async-start(f32[8,4,1024]{2,1,0:T(4,128)} %broadcast_in_dim.30), calls=%async_computation.3 | async-start | bytes 262144 | tf_op jit(solution)/shard_map/all_to_all | solution.py:20
  100.0 2.9 %collective-permute-start.1 = (f32[1024,64]{1,0:T(8,128)S(1)}, f32[1024,64]{1,0:T(8,128)S(1)}, u32[]{:S(2)}, u32[]{:S(2)}) collective-permute-start(f32[1024,64]{1,0:T(8,128)S(1)} %bitcast.226), channel_id=1, source_target_pairs={{0,16},{16,0},{1,17},{17,1},{2,18},{18,2},{3,19},{19,3},{4,20},{20... | collective-permute-start | bytes 786440 | tf_op jit(solution)/shard_map/ppermute | solution.py:80
  102.8 2.5 all-to-all-done.3
  108.7 4.8 %all-to-all-start.4 = ((f32[16,4,1024]{2,1,0:T(4,128)}), f32[16,4,1024]{2,1,0:T(4,128)}, u32[]{:S(2)}, u32[]{:S(2)}) async-start(f32[16,4,1024]{2,1,0:T(4,128)} %broadcast_in_dim.31), calls=%async_computation.4 | async-start | bytes 524288 | tf_op jit(solution)/shard_map/all_to_all | solution.py:20
  116.1 4.8 %all-to-all-done.4 = f32[16,4,1024]{2,1,0:T(4,128)} async-done(((f32[16,4,1024]{2,1,0:T(4,128)}), f32[16,4,1024]{2,1,0:T(4,128)}, u32[]{:S(2)}, u32[]{:S(2)}) %all-to-all-start.4) | async-done | bytes 262176 | tf_op jit(solution)/shard_map/all_to_all | solution.py:20
  120.9 1.6 bitcast_reduce_fusion
  123.8 3.6 %slice.324 = f32[1024,640]{1,0:T(8,128)} slice(f32[1024,768]{1,0:T(8,128)} %all-gather.2.cloned.1.call-done), slice={[0:1024], [0:640]} | slice | bytes 5242880 | tf_op jit(solution)/shard_map/slice | solution.py:129
  127.4 8.0 %collective-permute-start.3 = (f32[1024,640]{1,0:T(8,128)}, f32[1024,640]{1,0:T(8,128)}, u32[]{:S(2)}, u32[]{:S(2)}) collective-permute-start(f32[1024,640]{1,0:T(8,128)} %slice.324), channel_id=1, source_target_pairs={{0,16},{16,0},{1,17},{17,1},{2,18},{18,2},{3,19},{19,3},{4,20},{20... | collective-permute-start | bytes 7864328 | tf_op jit(solution)/shard_map/ppermute | solution.py:131
  135.5 1.9 collective-permute-start.2
  145.8 6.7 %all-to-all-start.5 = ((f32[16,4,1216]{2,1,0:T(4,128)}), f32[16,4,1216]{2,1,0:T(4,128)}, u32[]{:S(2)}, u32[]{:S(2)}) async-start(f32[16,4,1216]{2,1,0:T(4,128)} %pad_maximum_fusion.2), calls=%async_computation.5 | async-start | bytes 655360 | tf_op jit(solution)/shard_map/all_to_all | solution.py:20
  152.6 1.6 fusion.15
  155.3 5.3 %all-to-all-done.5 = f32[16,4,1216]{2,1,0:T(4,128)} async-done(((f32[16,4,1216]{2,1,0:T(4,128)}), f32[16,4,1216]{2,1,0:T(4,128)}, u32[]{:S(2)}, u32[]{:S(2)}) %all-to-all-start.5) | async-done | bytes 311328 | tf_op jit(solution)/shard_map/all_to_all | solution.py:20
  164.6 2.2 convolution_subtract_fusion.2
  168.0 1.6 convolution_add_fusion
  172.4 4.2 %all-to-all-start.6 = ((f32[16,4,512]{2,1,0:T(4,128)}), f32[16,4,512]{2,1,0:T(4,128)}, u32[]{:S(2)}, u32[]{:S(2)}) async-start(f32[16,4,512]{2,1,0:T(4,128)} %pad_maximum_fusion.4), calls=%async_computation.6 | async-start | bytes 262144 | tf_op jit(solution)/shard_map/all_to_all | solution.py:20
  178.3 4.9 %all-to-all-done.6 = f32[16,4,512]{2,1,0:T(4,128)} async-done(((f32[16,4,512]{2,1,0:T(4,128)}), f32[16,4,512]{2,1,0:T(4,128)}, u32[]{:S(2)}, u32[]{:S(2)}) %all-to-all-start.6) | async-done | bytes 131104 | tf_op jit(solution)/shard_map/all_to_all | solution.py:20
  183.3 1.6 fusion.88
  190.6 3.3 %all-to-all-start.7 = ((f32[8,4,384]{2,1,0:T(4,128)}), f32[8,4,384]{2,1,0:T(4,128)S(1)}, u32[]{:S(2)}, u32[]{:S(2)}) async-start(f32[8,4,384]{2,1,0:T(4,128)} %broadcast_in_dim.35), calls=%async_computation.7 | async-start | bytes 98304 | tf_op jit(solution)/shard_map/all_to_all | solution.py:20
  194.2 4.8 %all-to-all-done.7 = f32[8,4,384]{2,1,0:T(4,128)S(1)} async-done(((f32[8,4,384]{2,1,0:T(4,128)}), f32[8,4,384]{2,1,0:T(4,128)S(1)}, u32[]{:S(2)}, u32[]{:S(2)}) %all-to-all-start.7) | async-done | bytes 49184 | tf_op jit(solution)/shard_map/all_to_all | solution.py:20
  204.3 3.3 %all-to-all-start.8 = ((f32[4,4,768]{2,1,0:T(4,128)}), f32[4,4,768]{2,1,0:T(4,128)S(1)}, u32[]{:S(2)}, u32[]{:S(2)}) async-start(f32[4,4,768]{2,1,0:T(4,128)} %broadcast_in_dim.36), calls=%async_computation.8 | async-start | bytes 98304 | tf_op jit(solution)/shard_map/all_to_all | solution.py:20
  207.7 4.2 %all-to-all-done.8 = f32[4,4,768]{2,1,0:T(4,128)S(1)} async-done(((f32[4,4,768]{2,1,0:T(4,128)}), f32[4,4,768]{2,1,0:T(4,128)S(1)}, u32[]{:S(2)}, u32[]{:S(2)}) %all-to-all-start.8) | async-done | bytes 49184 | tf_op jit(solution)/shard_map/all_to_all | solution.py:20
  212.3 1.8 fusion.9
  214.0 1.7 fusion.5
  215.8 1.8 convolution_subtract_fusion.1
  217.5 1.8 broadcast_select_fusion.1
  219.8 26.3 %all_to_all.50 = f32[32,4,128]{2,1,0:T(4,128)S(1)} all-to-all(f32[32,4,128]{2,1,0:T(4,128)S(1)} %bitcast.240), channel_id=1, replica_groups=mesh['xh'=2,'xl'=2,'y'=4,'c'=2,'z'=16] {'c','z'}, dimensions={0} | all-to-all | bytes 131072 | tf_op jit(solution)/shard_map/all_to_all | solution.py:20
  (218 shorter events, 57.6 us)
Async XLA Ops:
  7.2 106.3 %copy-start = (f32[1024,128]{1,0:T(8,128)S(1)}, f32[1024,128]{1,0:T(8,128)}, u32[]{:S(2)}) copy-start(f32[1024,128]{1,0:T(8,128)} %param.20) | copy-start | bytes 1572868
  7.2 28.3 %copy-start.9 = (f32[2,64,64]{2,1,0:T(8,128)S(1)}, f32[2,64,64]{2,1,0:T(8,128)}, u32[]{:S(2)}) copy-start(f32[2,64,64]{2,1,0:T(8,128)} %param.12) | copy-start | bytes 98308
  7.2 28.3 %copy-start.4 = (f32[2,64,256]{2,1,0:T(8,128)S(1)}, f32[2,64,256]{2,1,0:T(8,128)}, u32[]{:S(2)}) copy-start(f32[2,64,256]{2,1,0:T(8,128)} %param.14) | copy-start | bytes 393220
  7.2 28.1 %copy-start.13 = (f32[2,64,32]{1,2,0:T(8,128)S(1)}, f32[2,64,32]{1,2,0:T(8,128)}, u32[]{:S(2)}) copy-start(f32[2,64,32]{1,2,0:T(8,128)} %param.11) | copy-start | bytes 49156
  10.7 15.0 %all-to-all-start.2 = ((f32[2,4,224]{2,1,0:T(4,128)}), f32[2,4,224]{2,1,0:T(4,128)S(1)}, u32[]{:S(2)}, u32[]{:S(2)}) async-start(f32[2,4,224]{2,1,0:T(4,128)} %pad_maximum_fusion.6), calls=%async_computation.2 | async-start | bytes 16384 | tf_op jit(solution)/shard_map/all_to_all | solution.py:20
  25.7 51.0 %all-to-all-start = ((f32[16,104,128]{2,1,0:T(8,128)}), f32[16,104,128]{2,1,0:T(8,128)S(1)}, u32[]{:S(2)}, u32[]{:S(2)}) async-start(f32[16,104,128]{2,1,0:T(8,128)} %pad_maximum_fusion), calls=%async_computation | async-start | bytes 1703936 | tf_op jit(solution)/shard_map/all_to_all | solution.py:20
  35.3 88.5 %all-gather.2.cloned.1.call-start = ((), (), s32[]{:S(2)}) async-start(), calls=%async_computation.10 | async-start | bytes 3342336 | tf_op jit(solution)/shard_map/all_gather | solution.py:49
  77.9 15.6 %all-to-all-start.1 = ((f32[8,4,1536]{2,1,0:T(4,128)}), f32[8,4,1536]{2,1,0:T(4,128)S(1)}, u32[]{:S(2)}, u32[]{:S(2)}) async-start(f32[8,4,1536]{2,1,0:T(4,128)} %pad_maximum_fusion.3), calls=%async_computation.1 | async-start | bytes 393216 | tf_op jit(solution)/shard_map/all_to_all | solution.py:20
  87.7 7.0 %collective-permute-start = (f32[1024,128]{1,0:T(8,128)S(1)}, f32[1024,128]{1,0:T(8,128)S(1)}, u32[]{:S(2)}, u32[]{:S(2)}) collective-permute-start(f32[1024,128]{1,0:T(8,128)S(1)} %bitcast.234), channel_id=1, source_target_pairs={{0,16},{16,0},{1,17},{17,1},{2,18},{18,2},{3,19},{19,3},{4,20},{20... | collective-permute-start | bytes 1572872 | tf_op jit(solution)/shard_map/ppermute | solution.py:79
  93.5 22.5 %copy-start.6 = (f32[2,4,1536]{2,1,0:T(4,128)}, f32[2,4,1536]{2,1,0:T(4,128)S(1)}, u32[]{:S(2)}) copy-start(f32[2,4,1536]{2,1,0:T(4,128)S(1)} %bitcast_reduce_fusion.1) | copy-start | bytes 147460
  94.1 5.8 %copy-start.12 = (f32[4,256]{1,0:T(4,128)}, f32[4,256]{1,0:T(4,128)S(1)}, u32[]{:S(2)}) copy-start(f32[4,256]{1,0:T(4,128)S(1)} %fusion.61) | copy-start | bytes 12292
  95.9 9.5 %all-to-all-start.3 = ((f32[8,4,1024]{2,1,0:T(4,128)}), f32[8,4,1024]{2,1,0:T(4,128)}, u32[]{:S(2)}, u32[]{:S(2)}) async-start(f32[8,4,1024]{2,1,0:T(4,128)} %broadcast_in_dim.30), calls=%async_computation.3 | async-start | bytes 262144 | tf_op jit(solution)/shard_map/all_to_all | solution.py:20
  100.0 7.3 %collective-permute-start.1 = (f32[1024,64]{1,0:T(8,128)S(1)}, f32[1024,64]{1,0:T(8,128)S(1)}, u32[]{:S(2)}, u32[]{:S(2)}) collective-permute-start(f32[1024,64]{1,0:T(8,128)S(1)} %bitcast.226), channel_id=1, source_target_pairs={{0,16},{16,0},{1,17},{17,1},{2,18},{18,2},{3,19},{19,3},{4,20},{20... | collective-permute-start | bytes 786440 | tf_op jit(solution)/shard_map/ppermute | solution.py:80
  106.8 30.6 %copy-start.10 = (f32[4,128]{1,0:T(4,128)}, f32[4,128]{1,0:T(4,128)S(1)}, u32[]{:S(2)}) copy-start(f32[4,128]{1,0:T(4,128)S(1)} %add.173) | copy-start | bytes 6148
  107.3 20.1 %copy-start.2 = (f32[1024,64]{1,0:T(8,128)}, f32[1024,64]{1,0:T(8,128)S(1)}, u32[]{:S(2)}) copy-start(f32[1024,64]{1,0:T(8,128)S(1)} %collective-permute-done.1) | copy-start | bytes 786436
  108.7 12.2 %all-to-all-start.4 = ((f32[16,4,1024]{2,1,0:T(4,128)}), f32[16,4,1024]{2,1,0:T(4,128)}, u32[]{:S(2)}, u32[]{:S(2)}) async-start(f32[16,4,1024]{2,1,0:T(4,128)} %broadcast_in_dim.31), calls=%async_computation.4 | async-start | bytes 524288 | tf_op jit(solution)/shard_map/all_to_all | solution.py:20
  123.7 14.9 %copy-start.11 = (f32[4,64]{1,0:T(4,128)}, f32[4,64]{1,0:T(4,128)S(1)}, u32[]{:S(2)}) copy-start(f32[4,64]{1,0:T(4,128)S(1)} %fusion.67) | copy-start | bytes 3076
  123.8 11.7 %copy-start.1 = (f32[1024,768]{1,0:T(8,128)S(1)}, f32[1024,768]{1,0:T(8,128)}, u32[]{:S(2)}) copy-start(f32[1024,768]{1,0:T(8,128)} %all-gather.2.cloned.1.call-done) | copy-start | bytes 9437188
  127.4 40.6 %collective-permute-start.3 = (f32[1024,640]{1,0:T(8,128)}, f32[1024,640]{1,0:T(8,128)}, u32[]{:S(2)}, u32[]{:S(2)}) collective-permute-start(f32[1024,640]{1,0:T(8,128)} %slice.324), channel_id=1, source_target_pairs={{0,16},{16,0},{1,17},{17,1},{2,18},{18,2},{3,19},{19,3},{4,20},{20... | collective-permute-start | bytes 7864328 | tf_op jit(solution)/shard_map/ppermute | solution.py:131
  135.5 5.2 %collective-permute-start.2 = (f32[1024,128]{1,0:T(8,128)S(1)}, f32[1024,128]{1,0:T(8,128)S(1)}, u32[]{:S(2)}, u32[]{:S(2)}) collective-permute-start(f32[1024,128]{1,0:T(8,128)S(1)} %slice.313), channel_id=1, source_target_pairs={{0,16},{16,0},{1,17},{17,1},{2,18},{18,2},{3,19},{19,3},{4,20},{20... | collective-permute-start | bytes 1572872 | tf_op jit(solution)/shard_map/ppermute | solution.py:130
  145.8 30.7 %slice-start = ((f32[2,4,1536]{2,1,0:T(4,128)}), f32[2,4,512]{2,1,0:T(4,128)S(1)}, s32[]{:S(2)}) async-start(f32[2,4,1536]{2,1,0:T(4,128)} %copy-done.6), calls=%async_computation.11 | async-start | bytes 32768 | tf_op jit(solution)/shard_map/slice | solution.py:104
  145.8 39.0 %copy-start.7 = (f32[4,16,64]{2,1,0:T(8,128)S(1)}, f32[4,16,64]{2,1,0:T(8,128)}, u32[]{:S(2)}) copy-start(f32[4,16,64]{2,1,0:T(8,128)} %copy.217) | copy-start | bytes 49156
  145.8 14.7 %all-to-all-start.5 = ((f32[16,4,1216]{2,1,0:T(4,128)}), f32[16,4,1216]{2,1,0:T(4,128)}, u32[]{:S(2)}, u32[]{:S(2)}) async-start(f32[16,4,1216]{2,1,0:T(4,128)} %pad_maximum_fusion.2), calls=%async_computation.5 | async-start | bytes 655360 | tf_op jit(solution)/shard_map/all_to_all | solution.py:20
  166.8 22.4 %copy-start.3 = (f32[1024,64]{1,0:T(8,128)S(1)}, f32[1024,64]{1,0:T(8,128)}, u32[]{:S(2)}) copy-start(f32[1024,64]{1,0:T(8,128)} %copy-done.2) | copy-start | bytes 786436
  167.3 0.7 copy-start.14
  167.3 0.7 copy-start.15
  172.4 10.9 %all-to-all-start.6 = ((f32[16,4,512]{2,1,0:T(4,128)}), f32[16,4,512]{2,1,0:T(4,128)}, u32[]{:S(2)}, u32[]{:S(2)}) async-start(f32[16,4,512]{2,1,0:T(4,128)} %pad_maximum_fusion.4), calls=%async_computation.6 | async-start | bytes 262144 | tf_op jit(solution)/shard_map/all_to_all | solution.py:20
  178.3 33.7 %copy-start.16 = (s32[16]{0:T(128)S(1)}, s32[16]{0:T(128)}, u32[]{:S(2)}) copy-start(s32[16]{0:T(128)} %get-tuple-element.48) | copy-start | bytes 196
  190.6 8.4 %all-to-all-start.7 = ((f32[8,4,384]{2,1,0:T(4,128)}), f32[8,4,384]{2,1,0:T(4,128)S(1)}, u32[]{:S(2)}, u32[]{:S(2)}) async-start(f32[8,4,384]{2,1,0:T(4,128)} %broadcast_in_dim.35), calls=%async_computation.7 | async-start | bytes 98304 | tf_op jit(solution)/shard_map/all_to_all | solution.py:20
  201.8 17.6 %copy-start.8 = (f32[16,4,64]{2,1,0:T(4,128)S(1)}, f32[16,4,64]{2,1,0:T(4,128)}, u32[]{:S(2)}) copy-start(f32[16,4,64]{2,1,0:T(4,128)} %get-tuple-element.32) | copy-start | bytes 49156
  201.8 17.7 %copy-start.5 = (f32[2,16,4,2]{3,2,1,0:T(4,128)S(1)}, f32[2,16,4,2]{3,2,1,0:T(4,128)}, u32[]{:S(2)}) copy-start(f32[2,16,4,2]{3,2,1,0:T(4,128)} %copy.205) | copy-start | bytes 3076
  204.3 7.6 %all-to-all-start.8 = ((f32[4,4,768]{2,1,0:T(4,128)}), f32[4,4,768]{2,1,0:T(4,128)S(1)}, u32[]{:S(2)}, u32[]{:S(2)}) async-start(f32[4,4,768]{2,1,0:T(4,128)} %broadcast_in_dim.36), calls=%async_computation.8 | async-start | bytes 98304 | tf_op jit(solution)/shard_map/all_to_all | solution.py:20
Sparse Core Ops, SparseCore 0:
  38.2 83.5 all-gather.1

commit v2 on v1

v2 whole, which is shorter than its diff:
```python
import jax
import jax.numpy as jnp
from jax import lax
from jax.experimental import pallas as pl
from jax.experimental.pallas import tpu as pltpu
from jax.sharding import Mesh, PartitionSpec as P

exact = lax.Precision.HIGHEST
LEAF = ("xh", "xl", "y", "c")
SWAP = [(0, 1), (1, 0)]


def dot_nt(left, right):
    return lax.dot_general(left, right, (((1,), (1,)), ((), ())), precision=exact)


def dot_nn(left, right):
    return lax.dot_general(left, right, (((1,), (0,)), ((), ())), precision=exact)


def exchange(value, axes):
    return lax.all_to_all(value, axes, 0, 0)


def to_all(value, count):
    return jnp.broadcast_to(value[None], (count,) + value.shape)


def shape(*dims):
    return jax.ShapeDtypeStruct(dims, jnp.float32)


def pack_panels(p0_ref, p1_ref, p2_ref, p3_ref, out_ref):
    out_ref[:, :256] = p3_ref[0]
    out_ref[:, 256:512] = p3_ref[1]
    out_ref[:, 512:640] = p2_ref[0]
    out_ref[:, 640:768] = jnp.concatenate([p1_ref[0], p1_ref[1]], 1)
    blank = jnp.zeros((64, 64), jnp.float32)
    out_ref[:, 768:] = jnp.concatenate([p0_ref[0], p0_ref[1], blank], 1)


def first_parts(panel_ref, load_ref, inflow_ref, out_ref):
    x = 2 * lax.axis_index("xh") + lax.axis_index("xl")
    y, c = lax.axis_index("y"), lax.axis_index("c")
    keep = dot_nn(panel_ref[0], load_ref[...])
    take = dot_nn(panel_ref[1], load_ref[...])
    border = inflow_ref[2 * x + (y >> 1)]
    first = jnp.where((y & 1) + c == 0, 1.0, 0.0)
    both = jnp.concatenate([keep, first * border - take], 0)
    out_ref[...] = both.T.reshape(16, 8, 128)


def last_rows(got_ref, *out_refs):
    rows = got_ref[...].reshape(128, 128).T
    for ref, start in zip(out_refs, (28, 24, 16, 0, 64)):
        ref[...] = rows[start : start + ref.shape[0]]


def on_device(
    panel_0,
    panel_1,
    panel_2,
    panel_3,
    load_0,
    load_1,
    load_2,
    load_3,
    inflow,
    above_solution,
    block_maps,
):
    xh, xl = lax.axis_index("xh"), lax.axis_index("xl")
    y, c, z = lax.axis_index("y"), lax.axis_index("c"), lax.axis_index("z")
    x = 2 * xh + xl
    y_low = y & 1
    front_3 = 2 * x + (y >> 1)

    rows = pl.pallas_call(pack_panels, out_shape=shape(64, 896))(
        panel_0, panel_1, panel_2, panel_3
    )
    gathered = lax.all_gather(rows, "z", axis=0, tiled=True)
    rows, panel_3, load_3, inflow = lax.optimization_barrier((rows, panel_3, load_3, inflow))

    payload = pl.pallas_call(first_parts, out_shape=shape(16, 8, 128))(panel_3, load_3, inflow)
    payload, loads, above_in = lax.optimization_barrier(
        (payload, (load_0, load_1, load_2), above_solution)
    )
    got = exchange(payload, "z")

    loads = jnp.concatenate(loads, 0)
    loads = lax.dynamic_slice_in_dim(loads, z * 8, 8, 1).T
    loads_mine, loads_sent = jnp.where(c == 0, loads[:4], loads[4:]), jnp.where(c == 0, loads[4:], loads[:4])
    loads_other = lax.ppermute(loads_sent, "c", SWAP)

    def by_core(own, other):
        return jnp.where(c == 0, own, other), jnp.where(c == 0, other, own)

    loads_low, loads_high = by_core(loads_mine, loads_other)
    load_0c = jnp.concatenate([loads_low[:, :32], loads_high[:, :32]], 1)
    load_1c = jnp.concatenate([loads_low[:, 32:96], loads_high[:, 32:96]], 1)
    load_2c = jnp.concatenate([loads_low[:, 96:], loads_high[:, 96:]], 1)
    above = lax.dynamic_slice_in_dim(above_in, z * 8, 8, 1).T

    couple_2 = lax.all_gather(panel_2[1], "z", axis=0, tiled=True)
    couple_2, got = lax.optimization_barrier((couple_2, got))
    couple_2o = lax.ppermute(couple_2, "c", SWAP)
    vec = got.reshape(16, 8, 2, 64).transpose(2, 1, 0, 3).reshape(2, 8, 1024)

    def chip_nt(vector, own, other):
        width = own.shape[1]
        low, high = vector[:, :width], vector[:, width:]
        mine, rest = jnp.where(c == 0, low, high), jnp.where(c == 0, high, low)
        return dot_nt(mine, own) + dot_nt(rest, other)

    u_send = vec[1].reshape(2, 4, 1024)
    u_send = jnp.broadcast_to(u_send[None], (4, 2, 4, 1024)).reshape(8, 4, 1024)
    y_send = vec[0].reshape(2, 4, 4, 256).transpose(2, 1, 0, 3).reshape(4, 4, 512)
    y_send = jnp.concatenate([y_send, y_send], 0)
    got = exchange(jnp.concatenate([u_send, y_send], 2), ("y", "c"))
    got = got.reshape(2, 4, 4, 1536).sum(1)
    update = got[..., :1024]
    y3_piece = lax.dynamic_index_in_dim(got[..., 1024:], y >> 1, 0, keepdims=False)
    y3_piece = jnp.concatenate([y3_piece[:, :256], y3_piece[:, 256:]], 0)

    def lifted(update, base, block, count):
        maps = lax.dynamic_slice_in_dim(block_maps, base, 2, 0).reshape(32)
        targets = block * count + jnp.arange(count, dtype=jnp.int32)
        targets = jnp.concatenate([targets, targets + 16])
        chosen = (maps[:, None] == targets[None, :]).astype(jnp.float32)
        blocks = update.reshape(2, 4, 16, 64).transpose(1, 0, 2, 3).reshape(4, 32, 64)
        placed = jnp.einsum("rnk,np->rpk", blocks, chosen, precision=exact)
        separator = placed[:, :count].reshape(4, count * 64)
        border = placed[:, count:].reshape(4, count * 64)
        whole = jnp.zeros((4, 1024), jnp.float32)
        border = lax.dynamic_update_slice_in_dim(whole, border, block * count * 64, 1)
        return separator, border

    separator, border = lifted(update, 6 + 2 * x, y, 4)
    b_2 = separator + load_2c
    update = border - chip_nt(b_2, couple_2, couple_2o)
    update = exchange(to_all(update, 8), ("xl", "y")).reshape(2, 4, 4, 1024).sum(1)

    gathered, update = lax.optimization_barrier((gathered, update))
    upper = gathered[:, 512:]
    upper_o = lax.ppermute(upper, "c", SWAP)
    pivot_2, pivot_2o = upper[:, :128], upper_o[:, :128]
    panel_1g, panel_1o = upper[:, 128:256], upper_o[:, 128:256]
    panel_0g, panel_0o = upper[:, 256:320], upper_o[:, 256:320]
    separator, border = lifted(update, 2 + 2 * xh, 4 * xl + y, 2)
    b_1 = separator + load_1c
    update = border - chip_nt(b_1, panel_1g[:, 64:], panel_1o[:, 64:])
    update = exchange(to_all(update, 16), ("xh", "xl", "y")).reshape(2, 8, 4, 1024).sum(1)

    separator, border = lifted(update, 0, 4 * x + y, 1)
    b_0 = separator + load_0c
    y0_part = chip_nt(b_0, panel_0g[:, :32], panel_0o[:, :32])
    u0_part = border - chip_nt(b_0, panel_0g[:, 32:], panel_0o[:, 32:])
    y1_part = chip_nt(b_1, panel_1g[:, :64], panel_1o[:, :64])
    y2_part = chip_nt(b_2, pivot_2, pivot_2o)
    u0_send = u0_part.reshape(4, 16, 64).transpose(1, 0, 2)
    y1_send = y1_part.reshape(4, 8, 128).transpose(1, 0, 2)
    y1_send = jnp.concatenate([y1_send, y1_send], 0)
    y2_send = y2_part.reshape(4, 4, 256).transpose(1, 0, 2)
    y2_send = to_all(y2_send, 4).reshape(16, 4, 256)
    payload = jnp.concatenate([to_all(y0_part, 16), y2_send, y1_send, u0_send], 2)
    got = exchange(payload, ("xh", "xl", "y"))
    y_0 = got[..., :1024].sum(0)
    u0_piece = got[..., 1408:].sum(0)
    y1_piece = got[..., 1280:1408].reshape(2, 8, 4, 128).sum(1)
    y1_piece = lax.dynamic_index_in_dim(y1_piece, xh, 0, keepdims=False)
    y2_piece = got[..., 1024:1280].reshape(4, 4, 4, 256).sum(1)
    y2_piece = lax.dynamic_index_in_dim(y2_piece, x, 0, keepdims=False)

    def taken(row, x_vec, s_vec):
        chosen_map = lax.dynamic_index_in_dim(block_maps, row, 0, keepdims=False)
        targets = jnp.arange(32, dtype=jnp.int32)
        chosen = (targets[:, None] == chosen_map[None, :]).astype(jnp.float32)
        stacked = jnp.concatenate([x_vec, s_vec], 1).reshape(8, 32, 64)
        return jnp.einsum("rqk,qn->rnk", stacked, chosen, precision=exact).reshape(8, 1024)

    def paired(y_vec, s_vec, panel):
        both = dot_nn(jnp.concatenate([y_vec, s_vec], 0), panel)
        rows, width = y_vec.shape[0], panel.shape[1] // 2
        return both[:rows, :width] - both[rows:, width:]

    above_mine = jnp.where(c == 0, above[:4], above[4:])
    own = paired(y_0, above_mine, panel_0g)
    other = paired(y_0, above_mine, panel_0o)
    x0_piece = jnp.concatenate(by_core(own, other), 1)
    same = jnp.concatenate([x0_piece, u0_piece, y1_piece], 1)
    got = exchange(to_all(same, 32), LEAF).reshape(16, 2, 4, 256)
    x_0 = got[..., :64].transpose(1, 2, 0, 3).reshape(8, 1024)
    u_0 = got[..., 64:128].transpose(1, 2, 0, 3).reshape(8, 1024)
    y_1 = got[..., 128:].reshape(2, 8, 2, 4, 128)
    y_1 = lax.dynamic_index_in_dim(y_1, xh, 0, keepdims=False)
    y_1 = y_1.transpose(1, 2, 0, 3).reshape(8, 1024)

    s_1 = taken(xh, x_0, above)
    x1_piece = paired(y_1, s_1, panel_1g)
    y2_piece = jnp.concatenate([y2_piece[:, :128], y2_piece[:, 128:]], 0)
    got = exchange(to_all(jnp.concatenate([x1_piece, y2_piece], 1), 16), ("xl", "y", "c"))
    x_1 = got[..., :64].transpose(1, 0, 2).reshape(8, 1024)
    y_2 = lax.dynamic_index_in_dim(
        got[..., 64:].reshape(2, 4, 2, 2, 4, 128), xl, 0, keepdims=False
    )
    y_2 = y_2.transpose(1, 3, 0, 2, 4).reshape(8, 1024)

    s_2 = taken(2 + x, x_1, s_1)
    x2_piece = dot_nn(y_2, pivot_2) - dot_nn(s_2, couple_2)
    got = exchange(to_all(jnp.concatenate([x2_piece, y3_piece], 1), 8), ("y", "c"))
    x_2 = got[..., :128].transpose(1, 0, 2).reshape(8, 1024)
    y_3 = lax.dynamic_index_in_dim(got[..., 128:].reshape(2, 4, 8, 256), y >> 1, 0, keepdims=False)
    y_3 = y_3.transpose(1, 0, 2).reshape(8, 1024)

    s_3 = taken(6 + front_3, x_2, s_2)
    x3_piece = paired(y_3, s_3, gathered[:, :512])

    def to_rows(piece):
        return piece.reshape(8, 16, -1).transpose(1, 0, 2)

    x0_own = lax.dynamic_slice_in_dim(x_0, 64 * (4 * x + y) + 32 * c, 32, 1)
    payload = jnp.concatenate(
        [
            to_rows(x3_piece),
            to_rows(x2_piece),
            to_rows(x1_piece),
            to_rows(x0_own),
            jnp.zeros((16, 8, 34), jnp.float32),
            u_0.reshape(8, 16, 64).transpose(1, 0, 2),
        ],
        2,
    )
    got = exchange(payload, "z")
    return pl.pallas_call(
        last_rows,
        out_shape=[shape(2, 128), shape(4, 128), shape(8, 128), shape(16, 128), shape(64, 128)],
    )(got)


def solution(mesh):
    fine = Mesh(mesh.devices.reshape(2, 2, 4, 2, 16), ("xh", "xl", "y", "c", "z"))
    panel = P(None, "z", LEAF)
    load = P(LEAF, None)
    in_specs = (panel,) * 4 + (load,) * 4 + (P(None, "z", None), P(), P())
    out_specs = (P(LEAF + ("z",), None),) * 4 + (P("z", None),)
    return jax.shard_map(
        on_device, mesh=fine, in_specs=in_specs, out_specs=out_specs, check_vma=False
    )
```

time: 260 us -> 214 us (0.82)
  waiting for transfers between devices: 70.9 us -> 40.9 us
  blocking collectives: 26.3 us -> 50.7 us
  local copies, waits for them, and re-layouts: 29.2 us -> 16.7 us
  matrix products: 33.3 us -> 21 us
  other arithmetic: 12.7 us -> 2.59 us
  starting transfers between devices: 70.4 us -> 60.8 us
  Pallas kernels: 0 us -> 5.4 us
    all_gather x0 -> x1, blocking collectives: none -> 31.6 us  [on_device(): couple_2 = lax.all_gather(panel_2[1], 'z', axis=0, tiled=True)]
    all_to_all x9 -> x8, waiting for transfers between devices: 69.5 us -> 40.8 us  [exchange(): return lax.all_to_all(value, axes, 0, 0)]
    dot_general x16 -> x6, matrix products: 18.4 us -> 7.61 us  [dot_nn(): lax.dot_general(left, right, (((1,), (0,)), ((), ())), precision=exact)]
    all_to_all x1, blocking collectives: 26.3 us -> 19.1 us  [exchange(): return lax.all_to_all(value, axes, 0, 0)]
    ppermute x3 -> x2, starting transfers between devices: 12.8 us -> 7.13 us  [the longest x1 4.28 us: on_device(): upper_o = lax.ppermute(upper, 'c', SWAP)]
    pallas_call x0 -> x3, Pallas kernels: none -> 5.4 us  [the longest x1 2.04 us: on_device(): pl.pallas_call(first_parts, out_shape=shape(16, 8, 128))]
    slice x24 -> x18, local copies, waits for them, and re-layouts: 8.75 us -> 3.97 us  [the longest x1 2.67 us: on_device(): upper = gathered[:, 512:]]
    all_to_all x9 -> x8, starting transfers between devices: 55.6 us -> 51.8 us  [exchange(): return lax.all_to_all(value, axes, 0, 0)]
  transfers between devices with their start and end apart: 14 -> 12, of which waited for: 9 -> 7; matrix products, arithmetic and copies ran while one was open for 15% -> 8% of each run, Pallas kernels for 0% -> 1%
where the time goes in v2:
time: 214 us; the launch traced here: 213 us
  starting transfers between devices  60.8 us (28%)
  blocking collectives  50.7 us (24%)
  waiting for transfers between devices  40.9 us (19%)
  matrix products  21 us (10%)
  local copies, waits for them, and re-layouts  16.7 us (8%)
  between operations  14.6 us (7%)
  Pallas kernels  5.4 us (3%)
  other arithmetic  2.59 us (1%)
    all_to_all x8, starting transfers between devices, exchange(): return lax.all_to_all(value, axes, 0, 0)  51.8 us
    all_to_all x8, waiting for transfers between devices, exchange(): return lax.all_to_all(value, axes, 0, 0)  40.8 us
    all_gather x1, blocking collectives, on_device(): couple_2 = lax.all_gather(panel_2[1], 'z', axis=0, tiled=True)  31.6 us
    all_to_all x1, blocking collectives, exchange(): return lax.all_to_all(value, axes, 0, 0)  19.1 us
    dot_general x12, matrix products, dot_nt(): lax.dot_general(left, right, (((1,), (1,)), ((), ())), precision=exact)  12.2 us
    dot_general x6, matrix products, dot_nn(): lax.dot_general(left, right, (((1,), (0,)), ((), ())), precision=exact)  7.61 us
  transfers between devices with their start and end apart: 12, of which 7 were waited for; matrix products, arithmetic and copies ran while one was open for 8% of the time, Pallas kernels for 1%

profile of v2, /device:TPU:1, one launch (start us, length us, event | category | flops | bytes accessed | tf_op | source)
XLA Modules:
  0.0 212.7 jit_solution(12045821725235628866)
XLA Ops:
  7.2 1.5 copy.140.p0_ref
  8.7 1.8 shard_map.146
  10.6 2.0 shard_map.147
  12.6 15.7 %all-to-all-start = ((f32[16,8,128]{2,1,0:T(8,128)}), f32[16,8,128]{2,1,0:T(8,128)S(1)}, u32[]{:S(2)}, u32[]{:S(2)}) async-start(f32[16,8,128]{2,1,0:T(8,128)} %shard_map.147), calls=%async_computation | async-start | bytes 131072 | tf_op jit(solution)/shard_map/all_to_all | solution.py:22
  31.1 2.9 %collective-permute-start = (f32[4,224]{1,0:T(4,128)S(1)}, f32[4,224]{1,0:T(4,128)S(1)}, u32[]{:S(2)}, u32[]{:S(2)}) collective-permute-start(f32[4,224]{1,0:T(4,128)S(1)} %slice_select_fusion.1), channel_id=1, source_target_pairs={{0,16},{16,0},{1,17},{17,1},{2,18},{18,2},{3,19},{19,3},{4,20},{20... | collective-permute-start | bytes 10760 | tf_op jit(solution)/shard_map/ppermute | solution.py:93
  35.7 31.6 %all-gather = f32[1,1024,128]{2,1,0:T(8,128)S(1)} all-gather(f32[1,64,128]{2,1,0:T(8,128)S(1)} %slice.217), channel_id=2, replica_groups=mesh['xh'=2,'xl'=2,'y'=4,'c'=2,'z'=16] {'z'}, dimensions={1}, use_global_device_ids=true | all-gather | bytes 557056 | tf_op jit(solution)/shard_map/all_gather | solution.py:104
  68.5 8.6 %all-to-all-start.1 = ((f32[8,4,1536]{2,1,0:T(4,128)}), f32[8,4,1536]{2,1,0:T(4,128)S(1)}, u32[]{:S(2)}, u32[]{:S(2)}) async-start(f32[8,4,1536]{2,1,0:T(4,128)} %maximum_maximum_fusion), calls=%async_computation.1 | async-start | bytes 393216 | tf_op jit(solution)/shard_map/all_to_all | solution.py:22
  77.3 1.9 collective-permute-start.1
  79.2 3.9 %all-to-all-done.1 = f32[8,4,1536]{2,1,0:T(4,128)S(1)} async-done(((f32[8,4,1536]{2,1,0:T(4,128)}), f32[8,4,1536]{2,1,0:T(4,128)S(1)}, u32[]{:S(2)}, u32[]{:S(2)}) %all-to-all-start.1) | async-done | bytes 196640 | tf_op jit(solution)/shard_map/all_to_all | solution.py:22
  85.3 3.5 %all-to-all-start.2 = ((f32[8,4,1024]{2,1,0:T(4,128)}), f32[8,4,1024]{2,1,0:T(4,128)S(1)}, u32[]{:S(2)}, u32[]{:S(2)}) async-start(f32[8,4,1024]{2,1,0:T(4,128)} %broadcast_in_dim.22), calls=%async_computation.2 | async-start | bytes 262144 | tf_op jit(solution)/shard_map/all_to_all | solution.py:22
  89.3 5.0 %all-to-all-done.2 = f32[8,4,1024]{2,1,0:T(4,128)S(1)} async-done(((f32[8,4,1024]{2,1,0:T(4,128)}), f32[8,4,1024]{2,1,0:T(4,128)S(1)}, u32[]{:S(2)}, u32[]{:S(2)}) %all-to-all-start.2) | async-done | bytes 131104 | tf_op jit(solution)/shard_map/all_to_all | solution.py:22
  94.3 2.7 %slice.236 = f32[1024,384]{1,0:T(8,128)} slice(f32[1024,896]{1,0:T(8,128)} %all-gather.3.cloned.1.call-done), slice={[0:1024], [512:896]} | slice | bytes 3145728 | tf_op jit(solution)/shard_map/slice | solution.py:144
  97.0 4.3 %collective-permute-start.2 = (f32[1024,384]{1,0:T(8,128)}, f32[1024,384]{1,0:T(8,128)S(1)}, u32[]{:S(2)}, u32[]{:S(2)}) collective-permute-start(f32[1024,384]{1,0:T(8,128)} %slice.236), channel_id=1, source_target_pairs={{0,16},{16,0},{1,17},{17,1},{2,18},{18,2},{3,19},{19,3},{4,20},{20... | collective-permute-start | bytes 4718600 | tf_op jit(solution)/shard_map/ppermute | solution.py:145
  102.1 1.6 fusion.27
  103.6 1.7 fusion.23
  105.3 1.6 fusion.19
  108.4 6.0 %all-to-all-start.3 = ((f32[16,4,1024]{2,1,0:T(4,128)}), f32[16,4,1024]{2,1,0:T(4,128)S(1)}, u32[]{:S(2)}, u32[]{:S(2)}) async-start(f32[16,4,1024]{2,1,0:T(4,128)} %broadcast_in_dim.23), calls=%async_computation.3 | async-start | bytes 524288 | tf_op jit(solution)/shard_map/all_to_all | solution.py:22
  115.5 6.7 %all-to-all-done.3 = f32[16,4,1024]{2,1,0:T(4,128)S(1)} async-done(((f32[16,4,1024]{2,1,0:T(4,128)}), f32[16,4,1024]{2,1,0:T(4,128)S(1)}, u32[]{:S(2)}, u32[]{:S(2)}) %all-to-all-start.3) | async-done | bytes 262176 | tf_op jit(solution)/shard_map/all_to_all | solution.py:22
  122.7 1.6 fusion.21
  124.2 1.7 fusion.17
  128.4 3.9 %all-to-all-start.4 = ((f32[16,4,1472]{2,1,0:T(4,128)}), f32[16,4,1472]{2,1,0:T(4,128)S(1)}, u32[]{:S(2)}, u32[]{:S(2)}) async-start(f32[16,4,1472]{2,1,0:T(4,128)} %pad_maximum_fusion), calls=%async_computation.4 | async-start | bytes 786432 | tf_op jit(solution)/shard_map/all_to_all | solution.py:22
  133.2 7.2 %all-to-all-done.4 = f32[16,4,1472]{2,1,0:T(4,128)S(1)} async-done(((f32[16,4,1472]{2,1,0:T(4,128)}), f32[16,4,1472]{2,1,0:T(4,128)S(1)}, u32[]{:S(2)}, u32[]{:S(2)}) %all-to-all-start.4) | async-done | bytes 376864 | tf_op jit(solution)/shard_map/all_to_all | solution.py:22
  143.2 6.4 %all-to-all-start.5 = ((f32[32,4,256]{2,1,0:T(4,128)}), f32[32,4,256]{2,1,0:T(4,128)S(1)}, u32[]{:S(2)}, u32[]{:S(2)}) async-start(f32[32,4,256]{2,1,0:T(4,128)} %broadcast_in_dim.26), calls=%async_computation.5 | async-start | bytes 262144 | tf_op jit(solution)/shard_map/all_to_all | solution.py:22
  149.6 7.7 %all-to-all-done.5 = f32[32,4,256]{2,1,0:T(4,128)S(1)} async-done(((f32[32,4,256]{2,1,0:T(4,128)}), f32[32,4,256]{2,1,0:T(4,128)S(1)}, u32[]{:S(2)}, u32[]{:S(2)}) %all-to-all-start.5) | async-done | bytes 131104 | tf_op jit(solution)/shard_map/all_to_all | solution.py:22
  157.8 1.4 fusion.13
  160.0 3.7 %all-to-all-start.6 = ((f32[16,8,192]{2,1,0:T(8,128)}), f32[16,8,192]{2,1,0:T(8,128)S(1)}, u32[]{:S(2)}, u32[]{:S(2)}) async-start(f32[16,8,192]{2,1,0:T(8,128)} %broadcast_in_dim.27), calls=%async_computation.6 | async-start | bytes 262144 | tf_op jit(solution)/shard_map/all_to_all | solution.py:22
  164.0 5.9 %all-to-all-done.6 = f32[16,8,192]{2,1,0:T(8,128)S(1)} async-done(((f32[16,8,192]{2,1,0:T(8,128)}), f32[16,8,192]{2,1,0:T(8,128)S(1)}, u32[]{:S(2)}, u32[]{:S(2)}) %all-to-all-start.6) | async-done | bytes 98336 | tf_op jit(solution)/shard_map/all_to_all | solution.py:22
  172.9 3.9 %all-to-all-start.7 = ((f32[8,8,384]{2,1,0:T(8,128)}), f32[8,8,384]{2,1,0:T(8,128)S(1)}, u32[]{:S(2)}, u32[]{:S(2)}) async-start(f32[8,8,384]{2,1,0:T(8,128)} %broadcast_in_dim.28), calls=%async_computation.7 | async-start | bytes 196608 | tf_op jit(solution)/shard_map/all_to_all | solution.py:22
  177.2 4.6 %all-to-all-done.7 = f32[8,8,384]{2,1,0:T(8,128)S(1)} async-done(((f32[8,8,384]{2,1,0:T(8,128)}), f32[8,8,384]{2,1,0:T(8,128)S(1)}, u32[]{:S(2)}, u32[]{:S(2)}) %all-to-all-start.7) | async-done | bytes 98336 | tf_op jit(solution)/shard_map/all_to_all | solution.py:22
  182.2 2.7 %fusion = f32[16,512]{1,0:T(8,128)S(1)} fusion(f32[1024,896]{1,0:T(8,128)} %all-gather.3.cloned.1.call-done, f32[8,1024]{1,0:T(8,128)S(1)} %reshape.195, f32[8,1024]{1,0:T(8,128)S(1)} %bitcast.176), kind=kOutput, calls=%fused_computation | convolution fusion | flops 100679680 | bytes 2195456 | tf_op jit(solution)/shard_map/dot_general | solution.py:18
  185.2 19.1 %all_to_all.45.got_ref = f32[16,8,128]{2,1,0:T(8,128)} all-to-all(f32[16,8,128]{2,1,0:T(8,128)S(1)} %concatenate.104), channel_id=1, replica_groups=mesh['xh'=2,'xl'=2,'y'=4,'c'=2,'z'=16] {'z'}, dimensions={0} | all-to-all | bytes 131072 | tf_op jit(solution)/shard_map/all_to_all | solution.py:22
  204.3 1.6 shard_map.148
  (149 shorter events, 23.9 us)
Async XLA Ops:
  7.2 81.9 %copy-start = (f32[1024,128]{1,0:T(8,128)S(1)}, f32[1024,128]{1,0:T(8,128)}, u32[]{:S(2)}) copy-start(f32[1024,128]{1,0:T(8,128)} %param.20) | copy-start | bytes 1572868
  7.2 87.1 %all-gather.3.cloned.1.call-start = ((), (), s32[]{:S(2)}) async-start(), calls=%async_computation.9 | async-start | bytes 3899392 | tf_op jit(solution)/shard_map/all_gather | solution.py:81
  12.6 54.7 %all-to-all-start = ((f32[16,8,128]{2,1,0:T(8,128)}), f32[16,8,128]{2,1,0:T(8,128)S(1)}, u32[]{:S(2)}, u32[]{:S(2)}) async-start(f32[16,8,128]{2,1,0:T(8,128)} %shard_map.147), calls=%async_computation | async-start | bytes 131072 | tf_op jit(solution)/shard_map/all_to_all | solution.py:22
  31.1 46.0 %collective-permute-start = (f32[4,224]{1,0:T(4,128)S(1)}, f32[4,224]{1,0:T(4,128)S(1)}, u32[]{:S(2)}, u32[]{:S(2)}) collective-permute-start(f32[4,224]{1,0:T(4,128)S(1)} %slice_select_fusion.1), channel_id=1, source_target_pairs={{0,16},{16,0},{1,17},{17,1},{2,18},{18,2},{3,19},{19,3},{4,20},{20... | collective-permute-start | bytes 10760 | tf_op jit(solution)/shard_map/ppermute | solution.py:93
  68.5 14.5 %all-to-all-start.1 = ((f32[8,4,1536]{2,1,0:T(4,128)}), f32[8,4,1536]{2,1,0:T(4,128)S(1)}, u32[]{:S(2)}, u32[]{:S(2)}) async-start(f32[8,4,1536]{2,1,0:T(4,128)} %maximum_maximum_fusion), calls=%async_computation.1 | async-start | bytes 393216 | tf_op jit(solution)/shard_map/all_to_all | solution.py:22
  77.3 6.8 %collective-permute-start.1 = (f32[1024,128]{1,0:T(8,128)S(1)}, f32[1024,128]{1,0:T(8,128)S(1)}, u32[]{:S(2)}, u32[]{:S(2)}) collective-permute-start(f32[1024,128]{1,0:T(8,128)S(1)} %bitcast.153), channel_id=1, source_target_pairs={{0,16},{16,0},{1,17},{17,1},{2,18},{18,2},{3,19},{19,3},{4,20},{20... | collective-permute-start | bytes 1572872 | tf_op jit(solution)/shard_map/ppermute | solution.py:106
  85.3 8.9 %all-to-all-start.2 = ((f32[8,4,1024]{2,1,0:T(4,128)}), f32[8,4,1024]{2,1,0:T(4,128)S(1)}, u32[]{:S(2)}, u32[]{:S(2)}) async-start(f32[8,4,1024]{2,1,0:T(4,128)} %broadcast_in_dim.22), calls=%async_computation.2 | async-start | bytes 262144 | tf_op jit(solution)/shard_map/all_to_all | solution.py:22
  97.0 9.9 %collective-permute-start.2 = (f32[1024,384]{1,0:T(8,128)}, f32[1024,384]{1,0:T(8,128)S(1)}, u32[]{:S(2)}, u32[]{:S(2)}) collective-permute-start(f32[1024,384]{1,0:T(8,128)} %slice.236), channel_id=1, source_target_pairs={{0,16},{16,0},{1,17},{17,1},{2,18},{18,2},{3,19},{19,3},{4,20},{20... | collective-permute-start | bytes 4718600 | tf_op jit(solution)/shard_map/ppermute | solution.py:145
  108.4 13.8 %all-to-all-start.3 = ((f32[16,4,1024]{2,1,0:T(4,128)}), f32[16,4,1024]{2,1,0:T(4,128)S(1)}, u32[]{:S(2)}, u32[]{:S(2)}) async-start(f32[16,4,1024]{2,1,0:T(4,128)} %broadcast_in_dim.23), calls=%async_computation.3 | async-start | bytes 524288 | tf_op jit(solution)/shard_map/all_to_all | solution.py:22
  128.4 12.0 %all-to-all-start.4 = ((f32[16,4,1472]{2,1,0:T(4,128)}), f32[16,4,1472]{2,1,0:T(4,128)S(1)}, u32[]{:S(2)}, u32[]{:S(2)}) async-start(f32[16,4,1472]{2,1,0:T(4,128)} %pad_maximum_fusion), calls=%async_computation.4 | async-start | bytes 786432 | tf_op jit(solution)/shard_map/all_to_all | solution.py:22
  143.2 14.1 %all-to-all-start.5 = ((f32[32,4,256]{2,1,0:T(4,128)}), f32[32,4,256]{2,1,0:T(4,128)S(1)}, u32[]{:S(2)}, u32[]{:S(2)}) async-start(f32[32,4,256]{2,1,0:T(4,128)} %broadcast_in_dim.26), calls=%async_computation.5 | async-start | bytes 262144 | tf_op jit(solution)/shard_map/all_to_all | solution.py:22
  160.0 9.9 %all-to-all-start.6 = ((f32[16,8,192]{2,1,0:T(8,128)}), f32[16,8,192]{2,1,0:T(8,128)S(1)}, u32[]{:S(2)}, u32[]{:S(2)}) async-start(f32[16,8,192]{2,1,0:T(8,128)} %broadcast_in_dim.27), calls=%async_computation.6 | async-start | bytes 262144 | tf_op jit(solution)/shard_map/all_to_all | solution.py:22
  172.9 8.9 %all-to-all-start.7 = ((f32[8,8,384]{2,1,0:T(8,128)}), f32[8,8,384]{2,1,0:T(8,128)S(1)}, u32[]{:S(2)}, u32[]{:S(2)}) async-start(f32[8,8,384]{2,1,0:T(8,128)} %broadcast_in_dim.28), calls=%async_computation.7 | async-start | bytes 196608 | tf_op jit(solution)/shard_map/all_to_all | solution.py:22
Sparse Core Ops, SparseCore 0:
  10.7 77.2 all-gather.2

commit v3 on v2

--- a/solution.py
+++ b/solution.py
@@ -30,13 +30,18 @@
     return jax.ShapeDtypeStruct(dims, jnp.float32)
 
 
-def pack_panels(p0_ref, p1_ref, p2_ref, p3_ref, out_ref):
+def pack_upper(p0_ref, p1_ref, p2_ref, out_ref):
+    blank = jnp.zeros((64, 64), jnp.float32)
+    out_ref[:, :128] = p2_ref[0]
+    out_ref[:, 128:256] = jnp.concatenate([p1_ref[0], p1_ref[1]], 1)
+    out_ref[:, 256:] = jnp.concatenate([p0_ref[0].T, p0_ref[1].T, blank], 1)
+
+
+def pack_lower(p2_ref, p3_ref, upper_ref, out_ref):
     out_ref[:, :256] = p3_ref[0]
     out_ref[:, 256:512] = p3_ref[1]
-    out_ref[:, 512:640] = p2_ref[0]
-    out_ref[:, 640:768] = jnp.concatenate([p1_ref[0], p1_ref[1]], 1)
-    blank = jnp.zeros((64, 64), jnp.float32)
-    out_ref[:, 768:] = jnp.concatenate([p0_ref[0], p0_ref[1], blank], 1)
+    out_ref[:, 512:640] = p2_ref[1]
+    out_ref[:, 640:] = upper_ref[:, :256]
 
 
 def first_parts(panel_ref, load_ref, inflow_ref, out_ref):
@@ -75,10 +80,10 @@
     y_low = y & 1
     front_3 = 2 * x + (y >> 1)
 
-    rows = pl.pallas_call(pack_panels, out_shape=shape(64, 896))(
-        panel_0, panel_1, panel_2, panel_3
-    )
-    gathered = lax.all_gather(rows, "z", axis=0, tiled=True)
+    rows = pl.pallas_call(pack_upper, out_shape=shape(64, 384))(
+        panel_0.transpose(0, 2, 1), panel_1, panel_2
+    )
+    upper = lax.all_gather(rows, "z", axis=0, tiled=True)
     rows, panel_3, load_3, inflow = lax.optimization_barrier((rows, panel_3, load_3, inflow))
 
     payload = pl.pallas_call(first_parts, out_shape=shape(16, 8, 128))(panel_3, load_3, inflow)
@@ -104,6 +109,9 @@
     couple_2 = lax.all_gather(panel_2[1], "z", axis=0, tiled=True)
     couple_2, got = lax.optimization_barrier((couple_2, got))
     couple_2o = lax.ppermute(couple_2, "c", SWAP)
+    lower, _ = lax.optimization_barrier((panel_3, got))
+    lower = pl.pallas_call(pack_lower, out_shape=shape(64, 896))(panel_2, lower, rows)
+    lower = lax.all_gather(lower, "z", axis=0, tiled=True)
     vec = got.reshape(16, 8, 2, 64).transpose(2, 1, 0, 3).reshape(2, 8, 1024)
 
     def chip_nt(vector, own, other):
@@ -138,14 +146,16 @@
     separator, border = lifted(update, 6 + 2 * x, y, 4)
     b_2 = separator + load_2c
     update = border - chip_nt(b_2, couple_2, couple_2o)
+    upper, _ = lax.optimization_barrier((upper, update))
+    upper_o = lax.ppermute(upper, "c", SWAP)
+
+    def split(value):
+        return lax.optimization_barrier((value[:, :128], value[:, 128:256], value[:, 256:320]))
+
+    pivot_2, panel_1g, panel_0g = split(upper)
+    pivot_2o, panel_1o, panel_0o = split(upper_o)
     update = exchange(to_all(update, 8), ("xl", "y")).reshape(2, 4, 4, 1024).sum(1)
 
-    gathered, update = lax.optimization_barrier((gathered, update))
-    upper = gathered[:, 512:]
-    upper_o = lax.ppermute(upper, "c", SWAP)
-    pivot_2, pivot_2o = upper[:, :128], upper_o[:, :128]
-    panel_1g, panel_1o = upper[:, 128:256], upper_o[:, 128:256]
-    panel_0g, panel_0o = upper[:, 256:320], upper_o[:, 256:320]
     separator, border = lifted(update, 2 + 2 * xh, 4 * xl + y, 2)
     b_1 = separator + load_1c
     update = border - chip_nt(b_1, panel_1g[:, 64:], panel_1o[:, 64:])
@@ -213,7 +223,7 @@
     y_3 = y_3.transpose(1, 0, 2).reshape(8, 1024)
 
     s_3 = taken(6 + front_3, x_2, s_2)
-    x3_piece = paired(y_3, s_3, gathered[:, :512])
+    x3_piece = paired(y_3, s_3, lower[:, :512])
 
     def to_rows(piece):
         return piece.reshape(8, 16, -1).transpose(1, 0, 2)

time: 214 us -> 207 us (0.967)
  matrix products: 21 us -> 14.4 us
  waiting for transfers between devices: 40.9 us -> 37.4 us
    all_to_all x8, starting transfers between devices: 51.8 us -> 45.4 us  [exchange(): return lax.all_to_all(value, axes, 0, 0)]
    ppermute x1, starting transfers between devices: 2.85 us -> 8.79 us  [on_device(): loads_other = lax.ppermute(loads_sent, 'c', SWAP)]
    dot_general x12, matrix products: 12.2 us -> 7.98 us  [dot_nt(): lax.dot_general(left, right, (((1,), (1,)), ((), ())), precision=exact)]
    all_to_all x8, waiting for transfers between devices: 40.8 us -> 37.4 us  [exchange(): return lax.all_to_all(value, axes, 0, 0)]
    dot_general x6, matrix products: 7.61 us -> 4.51 us  [dot_nn(): lax.dot_general(left, right, (((1,), (0,)), ((), ())), precision=exact)]
    slice x1 -> x4, local copies, waits for them, and re-layouts: 2.67 us -> 5.52 us  [the longest x2 3.37 us: split(): value[:, 128:256]]
  transfers between devices with their start and end apart: 12 -> 13, of which waited for: 7 -> 7; matrix products, arithmetic and copies ran while one was open for 8% -> 16% of each run, Pallas kernels for 1% -> 2%
where the time goes in v3:
time: 207 us; the launch traced here: 205 us
  starting transfers between devices  60.4 us (29%)
  blocking collectives  49.5 us (24%)
  waiting for transfers between devices  37.4 us (18%)
  local copies, waits for them, and re-layouts  18.6 us (9%)
  between operations  14.6 us (7%)
  matrix products  14.4 us (7%)
  Pallas kernels  7.03 us (3%)
  other arithmetic  3.11 us (2%)
    all_to_all x8, starting transfers between devices, exchange(): return lax.all_to_all(value, axes, 0, 0)  45.4 us
    all_to_all x8, waiting for transfers between devices, exchange(): return lax.all_to_all(value, axes, 0, 0)  37.4 us
    all_gather x1, blocking collectives, on_device(): couple_2 = lax.all_gather(panel_2[1], 'z', axis=0, tiled=True)  30.1 us
    all_to_all x1, blocking collectives, exchange(): return lax.all_to_all(value, axes, 0, 0)  19.4 us
    ppermute x1, starting transfers between devices, on_device(): loads_other = lax.ppermute(loads_sent, 'c', SWAP)  8.79 us
    dot_general x12, matrix products, dot_nt(): lax.dot_general(left, right, (((1,), (1,)), ((), ())), precision=exact)  7.98 us
    dot_general x6, matrix products, dot_nn(): lax.dot_general(left, right, (((1,), (0,)), ((), ())), precision=exact)  4.51 us
    ppermute x1, starting transfers between devices, on_device(): upper_o = lax.ppermute(upper, 'c', SWAP)  4.19 us
  transfers between devices with their start and end apart: 13, of which 7 were waited for; matrix products, arithmetic and copies ran while one was open for 16% of the time, Pallas kernels for 2%

profile of v3, /device:TPU:1, one launch (start us, length us, event | category | flops | bytes accessed | tf_op | source)
XLA Modules:
  0.0 205.0 jit_solution(11911692338137168414)
XLA Ops:
  7.2 1.7 shard_map.146.upper_ref
  9.0 2.0 shard_map.147
  12.7 0.9 copy.139
  13.7 8.8 %collective-permute-start = (f32[4,224]{1,0:T(4,128)S(1)}, f32[4,224]{1,0:T(4,128)S(1)}, u32[]{:S(2)}, u32[]{:S(2)}) collective-permute-start(f32[4,224]{1,0:T(4,128)S(1)} %slice_select_fusion.1), channel_id=1, source_target_pairs={{0,16},{16,0},{1,17},{17,1},{2,18},{18,2},{3,19},{19,3},{4,20},{20... | collective-permute-start | bytes 10760 | tf_op jit(solution)/shard_map/ppermute | solution.py:98
  22.5 9.5 %all-to-all-start = ((f32[16,8,128]{2,1,0:T(8,128)}), f32[16,8,128]{2,1,0:T(8,128)S(1)}, u32[]{:S(2)}, u32[]{:S(2)}) async-start(f32[16,8,128]{2,1,0:T(8,128)} %shard_map.147), calls=%async_computation | async-start | bytes 131072 | tf_op jit(solution)/shard_map/all_to_all | solution.py:22
  34.5 30.1 %all-gather = f32[1,1024,128]{2,1,0:T(8,128)S(1)} all-gather(f32[1,64,128]{2,1,0:T(8,128)S(1)} %slice.205), channel_id=2, replica_groups=mesh['xh'=2,'xl'=2,'y'=4,'c'=2,'z'=16] {'z'}, dimensions={1}, use_global_device_ids=true | all-gather | bytes 557056 | tf_op jit(solution)/shard_map/all_gather | solution.py:109
  65.8 9.8 %all-to-all-start.1 = ((f32[8,4,1536]{2,1,0:T(4,128)}), f32[8,4,1536]{2,1,0:T(4,128)S(1)}, u32[]{:S(2)}, u32[]{:S(2)}) async-start(f32[8,4,1536]{2,1,0:T(4,128)} %maximum_maximum_fusion), calls=%async_computation.1 | async-start | bytes 393216 | tf_op jit(solution)/shard_map/all_to_all | solution.py:22
  75.7 1.9 collective-permute-start.1
  77.6 3.9 %all-to-all-done.1 = f32[8,4,1536]{2,1,0:T(4,128)S(1)} async-done(((f32[8,4,1536]{2,1,0:T(4,128)}), f32[8,4,1536]{2,1,0:T(4,128)S(1)}, u32[]{:S(2)}, u32[]{:S(2)}) %all-to-all-start.1) | async-done | bytes 196640 | tf_op jit(solution)/shard_map/all_to_all | solution.py:22
  83.7 3.4 %all-to-all-start.2 = ((f32[8,4,1024]{2,1,0:T(4,128)}), f32[8,4,1024]{2,1,0:T(4,128)S(1)}, u32[]{:S(2)}, u32[]{:S(2)}) async-start(f32[8,4,1024]{2,1,0:T(4,128)} %broadcast_in_dim.22), calls=%async_computation.2 | async-start | bytes 262144 | tf_op jit(solution)/shard_map/all_to_all | solution.py:22
  88.2 1.7 shard_map.148
  90.0 2.5 %all-to-all-done.2 = f32[8,4,1024]{2,1,0:T(4,128)S(1)} async-done(((f32[8,4,1024]{2,1,0:T(4,128)}), f32[8,4,1024]{2,1,0:T(4,128)S(1)}, u32[]{:S(2)}, u32[]{:S(2)}) %all-to-all-start.2) | async-done | bytes 131104 | tf_op jit(solution)/shard_map/all_to_all | solution.py:22
  92.6 4.2 %collective-permute-start.2 = (f32[1024,384]{1,0:T(8,128)}, f32[1024,384]{1,0:T(8,128)}, u32[]{:S(2)}, u32[]{:S(2)}) collective-permute-start(f32[1024,384]{1,0:T(8,128)} %all-gather.4.cloned.1.call-done), channel_id=1, source_target_pairs={{0,16},{16,0},{1,17},{17,1},{2,18},{18,2},{3,19},{19,3},{4,20},{20... | collective-permute-start | bytes 4718600 | tf_op jit(solution)/shard_map/ppermute | solution.py:150
  97.3 1.1 slice.225
  98.4 1.3 fusion.76
  101.4 2.1 %fusion.75 = (f32[1024,128]{1,0:T(8,128)S(1)}, f32[1024,128]{1,0:T(8,128)}) fusion(f32[1024,384]{1,0:T(8,128)} %collective-permute-done.2), kind=kLoop, calls=%fused_computation.157 | loop fusion | bytes 2097152 | tf_op jit(solution)/shard_map/slice | solution.py:153
  103.5 1.1 slice.287
  106.0 4.8 %all-to-all-start.3 = ((f32[16,4,1024]{2,1,0:T(4,128)}), f32[16,4,1024]{2,1,0:T(4,128)S(1)}, u32[]{:S(2)}, u32[]{:S(2)}) async-start(f32[16,4,1024]{2,1,0:T(4,128)} %broadcast_in_dim.23), calls=%async_computation.3 | async-start | bytes 524288 | tf_op jit(solution)/shard_map/all_to_all | solution.py:22
  110.8 1.6 convolution_add_fusion.2
  113.0 5.7 %all-to-all-done.3 = f32[16,4,1024]{2,1,0:T(4,128)S(1)} async-done(((f32[16,4,1024]{2,1,0:T(4,128)}), f32[16,4,1024]{2,1,0:T(4,128)S(1)}, u32[]{:S(2)}, u32[]{:S(2)}) %all-to-all-start.3) | async-done | bytes 262176 | tf_op jit(solution)/shard_map/all_to_all | solution.py:22
  118.8 0.9 fusion.55
  123.4 4.0 %all-to-all-start.4 = ((f32[16,4,1472]{2,1,0:T(4,128)}), f32[16,4,1472]{2,1,0:T(4,128)S(1)}, u32[]{:S(2)}, u32[]{:S(2)}) async-start(f32[16,4,1472]{2,1,0:T(4,128)} %pad_maximum_fusion), calls=%async_computation.4 | async-start | bytes 786432 | tf_op jit(solution)/shard_map/all_to_all | solution.py:22
  128.3 7.2 %all-to-all-done.4 = f32[16,4,1472]{2,1,0:T(4,128)S(1)} async-done(((f32[16,4,1472]{2,1,0:T(4,128)}), f32[16,4,1472]{2,1,0:T(4,128)S(1)}, u32[]{:S(2)}, u32[]{:S(2)}) %all-to-all-start.4) | async-done | bytes 376864 | tf_op jit(solution)/shard_map/all_to_all | solution.py:22
  137.2 6.4 %all-to-all-start.5 = ((f32[32,4,256]{2,1,0:T(4,128)}), f32[32,4,256]{2,1,0:T(4,128)S(1)}, u32[]{:S(2)}, u32[]{:S(2)}) async-start(f32[32,4,256]{2,1,0:T(4,128)} %broadcast_in_dim.26), calls=%async_computation.5 | async-start | bytes 262144 | tf_op jit(solution)/shard_map/all_to_all | solution.py:22
  143.7 7.7 %all-to-all-done.5 = f32[32,4,256]{2,1,0:T(4,128)S(1)} async-done(((f32[32,4,256]{2,1,0:T(4,128)}), f32[32,4,256]{2,1,0:T(4,128)S(1)}, u32[]{:S(2)}, u32[]{:S(2)}) %all-to-all-start.5) | async-done | bytes 131104 | tf_op jit(solution)/shard_map/all_to_all | solution.py:22
  153.0 3.7 %all-to-all-start.6 = ((f32[16,8,192]{2,1,0:T(8,128)}), f32[16,8,192]{2,1,0:T(8,128)S(1)}, u32[]{:S(2)}, u32[]{:S(2)}) async-start(f32[16,8,192]{2,1,0:T(8,128)} %broadcast_in_dim.27), calls=%async_computation.6 | async-start | bytes 262144 | tf_op jit(solution)/shard_map/all_to_all | solution.py:22
  157.1 5.9 %all-to-all-done.6 = f32[16,8,192]{2,1,0:T(8,128)S(1)} async-done(((f32[16,8,192]{2,1,0:T(8,128)}), f32[16,8,192]{2,1,0:T(8,128)S(1)}, u32[]{:S(2)}, u32[]{:S(2)}) %all-to-all-start.6) | async-done | bytes 98336 | tf_op jit(solution)/shard_map/all_to_all | solution.py:22
  164.8 3.9 %all-to-all-start.7 = ((f32[8,8,384]{2,1,0:T(8,128)}), f32[8,8,384]{2,1,0:T(8,128)S(1)}, u32[]{:S(2)}, u32[]{:S(2)}) async-start(f32[8,8,384]{2,1,0:T(8,128)} %broadcast_in_dim.28), calls=%async_computation.7 | async-start | bytes 196608 | tf_op jit(solution)/shard_map/all_to_all | solution.py:22
  169.2 4.6 %all-to-all-done.7 = f32[8,8,384]{2,1,0:T(8,128)S(1)} async-done(((f32[8,8,384]{2,1,0:T(8,128)}), f32[8,8,384]{2,1,0:T(8,128)S(1)}, u32[]{:S(2)}, u32[]{:S(2)}) %all-to-all-start.7) | async-done | bytes 98336 | tf_op jit(solution)/shard_map/all_to_all | solution.py:22
  174.2 2.7 %fusion = f32[16,512]{1,0:T(8,128)S(1)} fusion(f32[1024,896]{1,0:T(8,128)} %all-gather.6.cloned.1.call-done, f32[8,1024]{1,0:T(8,128)S(1)} %reshape.195, f32[8,1024]{1,0:T(8,128)S(1)} %bitcast.183), kind=kOutput, calls=%fused_computation | convolution fusion | flops 100679680 | bytes 2195456 | tf_op jit(solution)/shard_map/dot_general | solution.py:18
  177.2 19.4 %all_to_all.45.got_ref = f32[16,8,128]{2,1,0:T(8,128)} all-to-all(f32[16,8,128]{2,1,0:T(8,128)S(1)} %concatenate.104), channel_id=1, replica_groups=mesh['xh'=2,'xl'=2,'y'=4,'c'=2,'z'=16] {'z'}, dimensions={0} | all-to-all | bytes 131072 | tf_op jit(solution)/shard_map/all_to_all | solution.py:22
  196.6 1.6 shard_map.149
  (155 shorter events, 24.7 us)
Async XLA Ops:
  7.2 85.5 %all-gather.4.cloned.1.call-start = ((), (), s32[]{:S(2)}) async-start(), calls=%async_computation.9 | async-start | bytes 1671168 | tf_op jit(solution)/shard_map/all_gather | solution.py:86
  13.7 61.8 %collective-permute-start = (f32[4,224]{1,0:T(4,128)S(1)}, f32[4,224]{1,0:T(4,128)S(1)}, u32[]{:S(2)}, u32[]{:S(2)}) collective-permute-start(f32[4,224]{1,0:T(4,128)S(1)} %slice_select_fusion.1), channel_id=1, source_target_pairs={{0,16},{16,0},{1,17},{17,1},{2,18},{18,2},{3,19},{19,3},{4,20},{20... | collective-permute-start | bytes 10760 | tf_op jit(solution)/shard_map/ppermute | solution.py:98
  22.5 42.0 %all-to-all-start = ((f32[16,8,128]{2,1,0:T(8,128)}), f32[16,8,128]{2,1,0:T(8,128)S(1)}, u32[]{:S(2)}, u32[]{:S(2)}) async-start(f32[16,8,128]{2,1,0:T(8,128)} %shard_map.147), calls=%async_computation | async-start | bytes 131072 | tf_op jit(solution)/shard_map/all_to_all | solution.py:22
  64.6 23.3 %copy-start = (f32[1024,128]{1,0:T(8,128)S(1)}, f32[1024,128]{1,0:T(8,128)}, u32[]{:S(2)}) copy-start(f32[1024,128]{1,0:T(8,128)} %param.20) | copy-start | bytes 1572868
  65.8 15.7 %all-to-all-start.1 = ((f32[8,4,1536]{2,1,0:T(4,128)}), f32[8,4,1536]{2,1,0:T(4,128)S(1)}, u32[]{:S(2)}, u32[]{:S(2)}) async-start(f32[8,4,1536]{2,1,0:T(4,128)} %maximum_maximum_fusion), calls=%async_computation.1 | async-start | bytes 393216 | tf_op jit(solution)/shard_map/all_to_all | solution.py:22
  75.7 6.8 %collective-permute-start.1 = (f32[1024,128]{1,0:T(8,128)S(1)}, f32[1024,128]{1,0:T(8,128)S(1)}, u32[]{:S(2)}, u32[]{:S(2)}) collective-permute-start(f32[1024,128]{1,0:T(8,128)S(1)} %bitcast.160), channel_id=1, source_target_pairs={{0,16},{16,0},{1,17},{17,1},{2,18},{18,2},{3,19},{19,3},{4,20},{20... | collective-permute-start | bytes 1572872 | tf_op jit(solution)/shard_map/ppermute | solution.py:111
  83.7 8.7 %all-to-all-start.2 = ((f32[8,4,1024]{2,1,0:T(4,128)}), f32[8,4,1024]{2,1,0:T(4,128)S(1)}, u32[]{:S(2)}, u32[]{:S(2)}) async-start(f32[8,4,1024]{2,1,0:T(4,128)} %broadcast_in_dim.22), calls=%async_computation.2 | async-start | bytes 262144 | tf_op jit(solution)/shard_map/all_to_all | solution.py:22
  87.1 87.1 %all-gather.6.cloned.1.call-start = ((), (), s32[]{:S(2)}) async-start(), calls=%async_computation.10 | async-start | bytes 3899392 | tf_op jit(solution)/shard_map/all_gather | solution.py:114
  92.6 8.8 %collective-permute-start.2 = (f32[1024,384]{1,0:T(8,128)}, f32[1024,384]{1,0:T(8,128)}, u32[]{:S(2)}, u32[]{:S(2)}) collective-permute-start(f32[1024,384]{1,0:T(8,128)} %all-gather.4.cloned.1.call-done), channel_id=1, source_target_pairs={{0,16},{16,0},{1,17},{17,1},{2,18},{18,2},{3,19},{19,3},{4,20},{20... | collective-permute-start | bytes 4718600 | tf_op jit(solution)/shard_map/ppermute | solution.py:150
  106.0 12.6 %all-to-all-start.3 = ((f32[16,4,1024]{2,1,0:T(4,128)}), f32[16,4,1024]{2,1,0:T(4,128)S(1)}, u32[]{:S(2)}, u32[]{:S(2)}) async-start(f32[16,4,1024]{2,1,0:T(4,128)} %broadcast_in_dim.23), calls=%async_computation.3 | async-start | bytes 524288 | tf_op jit(solution)/shard_map/all_to_all | solution.py:22
  123.4 12.1 %all-to-all-start.4 = ((f32[16,4,1472]{2,1,0:T(4,128)}), f32[16,4,1472]{2,1,0:T(4,128)S(1)}, u32[]{:S(2)}, u32[]{:S(2)}) async-start(f32[16,4,1472]{2,1,0:T(4,128)} %pad_maximum_fusion), calls=%async_computation.4 | async-start | bytes 786432 | tf_op jit(solution)/shard_map/all_to_all | solution.py:22
  137.2 14.1 %all-to-all-start.5 = ((f32[32,4,256]{2,1,0:T(4,128)}), f32[32,4,256]{2,1,0:T(4,128)S(1)}, u32[]{:S(2)}, u32[]{:S(2)}) async-start(f32[32,4,256]{2,1,0:T(4,128)} %broadcast_in_dim.26), calls=%async_computation.5 | async-start | bytes 262144 | tf_op jit(solution)/shard_map/all_to_all | solution.py:22
  153.0 9.9 %all-to-all-start.6 = ((f32[16,8,192]{2,1,0:T(8,128)}), f32[16,8,192]{2,1,0:T(8,128)S(1)}, u32[]{:S(2)}, u32[]{:S(2)}) async-start(f32[16,8,192]{2,1,0:T(8,128)} %broadcast_in_dim.27), calls=%async_computation.6 | async-start | bytes 262144 | tf_op jit(solution)/shard_map/all_to_all | solution.py:22
  164.8 8.9 %all-to-all-start.7 = ((f32[8,8,384]{2,1,0:T(8,128)}), f32[8,8,384]{2,1,0:T(8,128)S(1)}, u32[]{:S(2)}, u32[]{:S(2)}) async-start(f32[8,8,384]{2,1,0:T(8,128)} %broadcast_in_dim.28), calls=%async_computation.7 | async-start | bytes 196608 | tf_op jit(solution)/shard_map/all_to_all | solution.py:22
Sparse Core Ops, SparseCore 0:
  10.1 71.7 all-gather.3
  90.1 67.7 all-gather.5

commit v4 on v3

--- a/solution.py
+++ b/solution.py
@@ -87,13 +87,11 @@
     rows, panel_3, load_3, inflow = lax.optimization_barrier((rows, panel_3, load_3, inflow))
 
     payload = pl.pallas_call(first_parts, out_shape=shape(16, 8, 128))(panel_3, load_3, inflow)
-    payload, loads, above_in = lax.optimization_barrier(
-        (payload, (load_0, load_1, load_2), above_solution)
-    )
+    payload, lane = lax.optimization_barrier((payload, z * 8))
     got = exchange(payload, "z")
 
-    loads = jnp.concatenate(loads, 0)
-    loads = lax.dynamic_slice_in_dim(loads, z * 8, 8, 1).T
+    loads = jnp.concatenate([load_0, load_1, load_2], 0)
+    loads = lax.dynamic_slice_in_dim(loads, lane, 8, 1).T
     loads_mine, loads_sent = jnp.where(c == 0, loads[:4], loads[4:]), jnp.where(c == 0, loads[4:], loads[:4])
     loads_other = lax.ppermute(loads_sent, "c", SWAP)
 
@@ -104,7 +102,7 @@
     load_0c = jnp.concatenate([loads_low[:, :32], loads_high[:, :32]], 1)
     load_1c = jnp.concatenate([loads_low[:, 32:96], loads_high[:, 32:96]], 1)
     load_2c = jnp.concatenate([loads_low[:, 96:], loads_high[:, 96:]], 1)
-    above = lax.dynamic_slice_in_dim(above_in, z * 8, 8, 1).T
+    above = lax.dynamic_slice_in_dim(above_solution, lane, 8, 1).T
 
     couple_2 = lax.all_gather(panel_2[1], "z", axis=0, tiled=True)
     couple_2, got = lax.optimization_barrier((couple_2, got))

time: 207 us -> 209 us (level)
  waiting for transfers between devices: 37.4 us -> 31.2 us
  local copies, waits for them, and re-layouts: 18.6 us -> 23.3 us
  matrix products: 14.4 us -> 17.1 us
    all_to_all x8, starting transfers between devices: 45.4 us -> 51.9 us  [exchange(): return lax.all_to_all(value, axes, 0, 0)]
    all_to_all x8, waiting for transfers between devices: 37.4 us -> 31.2 us  [exchange(): return lax.all_to_all(value, axes, 0, 0)]
    ppermute x1, starting transfers between devices: 8.79 us -> 2.86 us  [on_device(): loads_other = lax.ppermute(loads_sent, 'c', SWAP)]
    unnamed x4 -> x20, local copies, waits for them, and re-layouts: 0.03 us -> 5.09 us
    optimization_barrier x4 -> x0, local copies, waits for them, and re-layouts: 2.79 us -> none  [on_device(): lax.optimization_barrier((payload, (load_0, load_1, load_2), above_soluti...]
  transfers between devices with their start and end apart: 13 -> 13, of which waited for: 7 -> 7; matrix products, arithmetic and copies ran while one was open for 16% -> 20% of each run, Pallas kernels for 2% -> 2%
where the time goes in v4:
time: 209 us; the launch traced here: 207 us
  starting transfers between devices  60.8 us (29%)
  blocking collectives  48.8 us (23%)
  waiting for transfers between devices  31.2 us (15%)
  local copies, waits for them, and re-layouts  23.3 us (11%)
  matrix products  17.1 us (8%)
  between operations  14.6 us (7%)
  Pallas kernels  7.06 us (3%)
  other arithmetic  4.02 us (2%)
    all_to_all x8, starting transfers between devices, exchange(): return lax.all_to_all(value, axes, 0, 0)  51.9 us
    all_to_all x8, waiting for transfers between devices, exchange(): return lax.all_to_all(value, axes, 0, 0)  31.2 us
    all_gather x1, blocking collectives, on_device(): couple_2 = lax.all_gather(panel_2[1], 'z', axis=0, tiled=True)  30.4 us
    all_to_all x1, blocking collectives, exchange(): return lax.all_to_all(value, axes, 0, 0)  18.4 us
    dot_general x12, matrix products, dot_nt(): lax.dot_general(left, right, (((1,), (1,)), ((), ())), precision=exact)  9.04 us
    dot_general x6, matrix products, dot_nn(): lax.dot_general(left, right, (((1,), (0,)), ((), ())), precision=exact)  5.95 us
    unnamed x20, local copies, waits for them, and re-layouts  5.09 us
  transfers between devices with their start and end apart: 13, of which 7 were waited for; matrix products, arithmetic and copies ran while one was open for 20% of the time, Pallas kernels for 2%

profile of v4, /device:TPU:1, one launch (start us, length us, event | category | flops | bytes accessed | tf_op | source)
XLA Modules:
  0.0 206.9 jit_solution(12377504850618033351)
XLA Ops:
  7.2 1.8 shard_map.146.upper_ref
  9.0 2.0 shard_map.147
  11.1 15.7 %all-to-all-start = ((f32[16,8,128]{2,1,0:T(8,128)}), f32[16,8,128]{2,1,0:T(8,128)S(1)}, u32[]{:S(2)}, u32[]{:S(2)}) async-start(f32[16,8,128]{2,1,0:T(8,128)} %shard_map.147), calls=%async_computation | async-start | bytes 131072 | tf_op jit(solution)/shard_map/all_to_all | solution.py:22
  29.5 2.9 %collective-permute-start = (f32[4,224]{1,0:T(4,128)S(1)}, f32[4,224]{1,0:T(4,128)S(1)}, u32[]{:S(2)}, u32[]{:S(2)}) collective-permute-start(f32[4,224]{1,0:T(4,128)S(1)} %slice_select_fusion.1), channel_id=1, source_target_pairs={{0,16},{16,0},{1,17},{17,1},{2,18},{18,2},{3,19},{19,3},{4,20},{20... | collective-permute-start | bytes 10760 | tf_op jit(solution)/shard_map/ppermute | solution.py:96
  34.4 30.4 %all-gather = f32[1,1024,128]{2,1,0:T(8,128)S(1)} all-gather(f32[1,64,128]{2,1,0:T(8,128)S(1)} %slice-done), channel_id=2, replica_groups=mesh['xh'=2,'xl'=2,'y'=4,'c'=2,'z'=16] {'z'}, dimensions={1}, use_global_device_ids=true | all-gather | bytes 557056 | tf_op jit(solution)/shard_map/all_gather | solution.py:107
  66.0 9.1 %all-to-all-start.1 = ((f32[8,4,1536]{2,1,0:T(4,128)}), f32[8,4,1536]{2,1,0:T(4,128)S(1)}, u32[]{:S(2)}, u32[]{:S(2)}) async-start(f32[8,4,1536]{2,1,0:T(4,128)} %maximum_maximum_fusion), calls=%async_computation.1 | async-start | bytes 393216 | tf_op jit(solution)/shard_map/all_to_all | solution.py:22
  75.2 1.9 collective-permute-start.1
  77.1 3.8 %all-to-all-done.1 = f32[8,4,1536]{2,1,0:T(4,128)S(1)} async-done(((f32[8,4,1536]{2,1,0:T(4,128)}), f32[8,4,1536]{2,1,0:T(4,128)S(1)}, u32[]{:S(2)}, u32[]{:S(2)}) %all-to-all-start.1) | async-done | bytes 196640 | tf_op jit(solution)/shard_map/all_to_all | solution.py:22
  83.8 3.4 %all-to-all-start.2 = ((f32[8,4,1024]{2,1,0:T(4,128)}), f32[8,4,1024]{2,1,0:T(4,128)S(1)}, u32[]{:S(2)}, u32[]{:S(2)}) async-start(f32[8,4,1024]{2,1,0:T(4,128)} %broadcast_in_dim.22), calls=%async_computation.2 | async-start | bytes 262144 | tf_op jit(solution)/shard_map/all_to_all | solution.py:22
  87.7 1.7 shard_map.148
  89.5 3.2 %all-to-all-done.2 = f32[8,4,1024]{2,1,0:T(4,128)S(1)} async-done(((f32[8,4,1024]{2,1,0:T(4,128)}), f32[8,4,1024]{2,1,0:T(4,128)S(1)}, u32[]{:S(2)}, u32[]{:S(2)}) %all-to-all-start.2) | async-done | bytes 131104 | tf_op jit(solution)/shard_map/all_to_all | solution.py:22
  92.8 4.0 %collective-permute-start.2 = (f32[1024,384]{1,0:T(8,128)}, f32[1024,384]{1,0:T(8,128)}, u32[]{:S(2)}, u32[]{:S(2)}) collective-permute-start(f32[1024,384]{1,0:T(8,128)} %all-gather.4.cloned.1.call-done), channel_id=1, source_target_pairs={{0,16},{16,0},{1,17},{17,1},{2,18},{18,2},{3,19},{19,3},{4,20},{20... | collective-permute-start | bytes 4718600 | tf_op jit(solution)/shard_map/ppermute | solution.py:148
  101.3 2.1 %fusion.75 = (f32[1024,128]{1,0:T(8,128)S(1)}, f32[1024,128]{1,0:T(8,128)}) fusion(f32[1024,384]{1,0:T(8,128)} %collective-permute-done.2), kind=kLoop, calls=%fused_computation.157 | loop fusion | bytes 2097152 | tf_op jit(solution)/shard_map/slice | solution.py:151
  106.2 5.1 %all-to-all-start.3 = ((f32[16,4,1024]{2,1,0:T(4,128)}), f32[16,4,1024]{2,1,0:T(4,128)S(1)}, u32[]{:S(2)}, u32[]{:S(2)}) async-start(f32[16,4,1024]{2,1,0:T(4,128)} %broadcast_in_dim.23), calls=%async_computation.3 | async-start | bytes 524288 | tf_op jit(solution)/shard_map/all_to_all | solution.py:22
  111.3 1.6 convolution_add_fusion.2
  112.9 1.6 fusion.3
  114.5 4.6 %all-to-all-done.3 = f32[16,4,1024]{2,1,0:T(4,128)S(1)} async-done(((f32[16,4,1024]{2,1,0:T(4,128)}), f32[16,4,1024]{2,1,0:T(4,128)S(1)}, u32[]{:S(2)}, u32[]{:S(2)}) %all-to-all-start.3) | async-done | bytes 262176 | tf_op jit(solution)/shard_map/all_to_all | solution.py:22
  123.2 3.9 %all-to-all-start.4 = ((f32[16,4,1472]{2,1,0:T(4,128)}), f32[16,4,1472]{2,1,0:T(4,128)S(1)}, u32[]{:S(2)}, u32[]{:S(2)}) async-start(f32[16,4,1472]{2,1,0:T(4,128)} %pad_maximum_fusion), calls=%async_computation.4 | async-start | bytes 786432 | tf_op jit(solution)/shard_map/all_to_all | solution.py:22
  127.1 1.3 fusion.63
  128.4 1.8 copy.171
  130.2 1.4 concatenate.93
  131.7 1.4 slice_select_fusion
  133.7 1.5 all-to-all-done.4
  138.4 7.1 %all-to-all-start.5 = ((f32[32,4,256]{2,1,0:T(4,128)}), f32[32,4,256]{2,1,0:T(4,128)S(1)}, u32[]{:S(2)}, u32[]{:S(2)}) async-start(f32[32,4,256]{2,1,0:T(4,128)} %broadcast_in_dim.26), calls=%async_computation.5 | async-start | bytes 262144 | tf_op jit(solution)/shard_map/all_to_all | solution.py:22
  145.6 7.7 %all-to-all-done.5 = f32[32,4,256]{2,1,0:T(4,128)S(1)} async-done(((f32[32,4,256]{2,1,0:T(4,128)}), f32[32,4,256]{2,1,0:T(4,128)S(1)}, u32[]{:S(2)}, u32[]{:S(2)}) %all-to-all-start.5) | async-done | bytes 131104 | tf_op jit(solution)/shard_map/all_to_all | solution.py:22
  155.8 3.7 %all-to-all-start.6 = ((f32[16,8,192]{2,1,0:T(8,128)}), f32[16,8,192]{2,1,0:T(8,128)S(1)}, u32[]{:S(2)}, u32[]{:S(2)}) async-start(f32[16,8,192]{2,1,0:T(8,128)} %broadcast_in_dim.27), calls=%async_computation.6 | async-start | bytes 262144 | tf_op jit(solution)/shard_map/all_to_all | solution.py:22
  159.8 5.9 %all-to-all-done.6 = f32[16,8,192]{2,1,0:T(8,128)S(1)} async-done(((f32[16,8,192]{2,1,0:T(8,128)}), f32[16,8,192]{2,1,0:T(8,128)S(1)}, u32[]{:S(2)}, u32[]{:S(2)}) %all-to-all-start.6) | async-done | bytes 98336 | tf_op jit(solution)/shard_map/all_to_all | solution.py:22
  167.6 3.9 %all-to-all-start.7 = ((f32[8,8,384]{2,1,0:T(8,128)}), f32[8,8,384]{2,1,0:T(8,128)S(1)}, u32[]{:S(2)}, u32[]{:S(2)}) async-start(f32[8,8,384]{2,1,0:T(8,128)} %broadcast_in_dim.28), calls=%async_computation.7 | async-start | bytes 196608 | tf_op jit(solution)/shard_map/all_to_all | solution.py:22
  172.0 4.6 %all-to-all-done.7 = f32[8,8,384]{2,1,0:T(8,128)S(1)} async-done(((f32[8,8,384]{2,1,0:T(8,128)}), f32[8,8,384]{2,1,0:T(8,128)S(1)}, u32[]{:S(2)}, u32[]{:S(2)}) %all-to-all-start.7) | async-done | bytes 98336 | tf_op jit(solution)/shard_map/all_to_all | solution.py:22
  177.0 2.7 %fusion = f32[16,512]{1,0:T(8,128)S(1)} fusion(f32[1024,896]{1,0:T(8,128)} %all-gather.6.cloned.1.call-done, f32[8,1024]{1,0:T(8,128)S(1)} %reshape.195, f32[8,1024]{1,0:T(8,128)S(1)} %bitcast.184), kind=kOutput, calls=%fused_computation | convolution fusion | flops 100679680 | bytes 2195456 | tf_op jit(solution)/shard_map/dot_general | solution.py:18
  180.0 18.4 %all_to_all.45.got_ref = f32[16,8,128]{2,1,0:T(8,128)} all-to-all(f32[16,8,128]{2,1,0:T(8,128)S(1)} %concatenate.104), channel_id=1, replica_groups=mesh['xh'=2,'xl'=2,'y'=4,'c'=2,'z'=16] {'z'}, dimensions={0} | all-to-all | bytes 131072 | tf_op jit(solution)/shard_map/all_to_all | solution.py:22
  198.5 1.6 shard_map.149
  (169 shorter events, 30.5 us)
Async XLA Ops:
  7.2 26.2 %copy-start = (f32[1024,128]{1,0:T(8,128)S(1)}, f32[1024,128]{1,0:T(8,128)}, u32[]{:S(2)}) copy-start(f32[1024,128]{1,0:T(8,128)} %param.20) | copy-start | bytes 1572868
  7.2 27.2 %slice-start = ((f32[2,64,128]{2,1,0:T(8,128)}), f32[1,64,128]{2,1,0:T(8,128)S(1)}, s32[]{:S(2)}) async-start(f32[2,64,128]{2,1,0:T(8,128)} %p2_ref.3), calls=%async_computation.11 | async-start | bytes 65536 | tf_op jit(solution)/shard_map/slice | solution.py:107
  7.2 85.6 %all-gather.4.cloned.1.call-start = ((), (), s32[]{:S(2)}) async-start(), calls=%async_computation.9 | async-start | bytes 1671168 | tf_op jit(solution)/shard_map/all_gather | solution.py:86
  11.1 53.7 %all-to-all-start = ((f32[16,8,128]{2,1,0:T(8,128)}), f32[16,8,128]{2,1,0:T(8,128)S(1)}, u32[]{:S(2)}, u32[]{:S(2)}) async-start(f32[16,8,128]{2,1,0:T(8,128)} %shard_map.147), calls=%async_computation | async-start | bytes 131072 | tf_op jit(solution)/shard_map/all_to_all | solution.py:22
  29.5 45.5 %collective-permute-start = (f32[4,224]{1,0:T(4,128)S(1)}, f32[4,224]{1,0:T(4,128)S(1)}, u32[]{:S(2)}, u32[]{:S(2)}) collective-permute-start(f32[4,224]{1,0:T(4,128)S(1)} %slice_select_fusion.1), channel_id=1, source_target_pairs={{0,16},{16,0},{1,17},{17,1},{2,18},{18,2},{3,19},{19,3},{4,20},{20... | collective-permute-start | bytes 10760 | tf_op jit(solution)/shard_map/ppermute | solution.py:96
  66.0 15.0 %all-to-all-start.1 = ((f32[8,4,1536]{2,1,0:T(4,128)}), f32[8,4,1536]{2,1,0:T(4,128)S(1)}, u32[]{:S(2)}, u32[]{:S(2)}) async-start(f32[8,4,1536]{2,1,0:T(4,128)} %maximum_maximum_fusion), calls=%async_computation.1 | async-start | bytes 393216 | tf_op jit(solution)/shard_map/all_to_all | solution.py:22
  75.2 7.4 %collective-permute-start.1 = (f32[1024,128]{1,0:T(8,128)S(1)}, f32[1024,128]{1,0:T(8,128)S(1)}, u32[]{:S(2)}, u32[]{:S(2)}) collective-permute-start(f32[1024,128]{1,0:T(8,128)S(1)} %bitcast.159), channel_id=1, source_target_pairs={{0,16},{16,0},{1,17},{17,1},{2,18},{18,2},{3,19},{19,3},{4,20},{20... | collective-permute-start | bytes 1572872 | tf_op jit(solution)/shard_map/ppermute | solution.py:109
  81.0 0.6 copy-start.2
  83.8 8.8 %all-to-all-start.2 = ((f32[8,4,1024]{2,1,0:T(4,128)}), f32[8,4,1024]{2,1,0:T(4,128)S(1)}, u32[]{:S(2)}, u32[]{:S(2)}) async-start(f32[8,4,1024]{2,1,0:T(4,128)} %broadcast_in_dim.22), calls=%async_computation.2 | async-start | bytes 262144 | tf_op jit(solution)/shard_map/all_to_all | solution.py:22
  87.2 89.8 %all-gather.6.cloned.1.call-start = ((), (), s32[]{:S(2)}) async-start(), calls=%async_computation.10 | async-start | bytes 3899392 | tf_op jit(solution)/shard_map/all_gather | solution.py:112
  92.8 8.6 %collective-permute-start.2 = (f32[1024,384]{1,0:T(8,128)}, f32[1024,384]{1,0:T(8,128)}, u32[]{:S(2)}, u32[]{:S(2)}) collective-permute-start(f32[1024,384]{1,0:T(8,128)} %all-gather.4.cloned.1.call-done), channel_id=1, source_target_pairs={{0,16},{16,0},{1,17},{17,1},{2,18},{18,2},{3,19},{19,3},{4,20},{20... | collective-permute-start | bytes 4718600 | tf_op jit(solution)/shard_map/ppermute | solution.py:148
  103.4 1.3 copy-start.1
  106.2 13.0 %all-to-all-start.3 = ((f32[16,4,1024]{2,1,0:T(4,128)}), f32[16,4,1024]{2,1,0:T(4,128)S(1)}, u32[]{:S(2)}, u32[]{:S(2)}) async-start(f32[16,4,1024]{2,1,0:T(4,128)} %broadcast_in_dim.23), calls=%async_computation.3 | async-start | bytes 524288 | tf_op jit(solution)/shard_map/all_to_all | solution.py:22
  121.0 12.1 %slice-start.1 = ((f32[2,4,1536]{2,1,0:T(4,128)}), f32[2,4,512]{2,1,0:T(4,128)S(1)}, s32[]{:S(2)}) async-start(f32[2,4,1536]{2,1,0:T(4,128)} %copy-done.2), calls=%async_computation.12 | async-start | bytes 32768 | tf_op jit(solution)/shard_map/slice | solution.py:128
  123.2 12.0 %all-to-all-start.4 = ((f32[16,4,1472]{2,1,0:T(4,128)}), f32[16,4,1472]{2,1,0:T(4,128)S(1)}, u32[]{:S(2)}, u32[]{:S(2)}) async-start(f32[16,4,1472]{2,1,0:T(4,128)} %pad_maximum_fusion), calls=%async_computation.4 | async-start | bytes 786432 | tf_op jit(solution)/shard_map/all_to_all | solution.py:22
  133.7 19.6 %copy-start.6 = (s32[16]{0:T(128)S(1)}, s32[16]{0:T(128)}, u32[]{:S(2)}) copy-start(s32[16]{0:T(128)} %get-tuple-element.50) | copy-start | bytes 196
  133.7 25.7 %copy-start.3 = (f32[4,512]{1,0:T(4,128)S(1)}, f32[4,512]{1,0:T(4,128)}, u32[]{:S(2)}) copy-start(f32[4,512]{1,0:T(4,128)} %dynamic-slice_bitcast_fusion) | copy-start | bytes 24580
  136.4 29.5 %copy-start.5 = (s32[16]{0:T(128)S(1)}, s32[16]{0:T(128)}, u32[]{:S(2)}) copy-start(s32[16]{0:T(128)} %get-tuple-element.51) | copy-start | bytes 196
  138.4 14.8 %all-to-all-start.5 = ((f32[32,4,256]{2,1,0:T(4,128)}), f32[32,4,256]{2,1,0:T(4,128)S(1)}, u32[]{:S(2)}, u32[]{:S(2)}) async-start(f32[32,4,256]{2,1,0:T(4,128)} %broadcast_in_dim.26), calls=%async_computation.5 | async-start | bytes 262144 | tf_op jit(solution)/shard_map/all_to_all | solution.py:22
  154.6 22.1 %copy-start.4 = (s32[16]{0:T(128)S(1)}, s32[16]{0:T(128)}, u32[]{:S(2)}) copy-start(s32[16]{0:T(128)} %get-tuple-element.49) | copy-start | bytes 196
  155.8 9.9 %all-to-all-start.6 = ((f32[16,8,192]{2,1,0:T(8,128)}), f32[16,8,192]{2,1,0:T(8,128)S(1)}, u32[]{:S(2)}, u32[]{:S(2)}) async-start(f32[16,8,192]{2,1,0:T(8,128)} %broadcast_in_dim.27), calls=%async_computation.6 | async-start | bytes 262144 | tf_op jit(solution)/shard_map/all_to_all | solution.py:22
  167.6 8.9 %all-to-all-start.7 = ((f32[8,8,384]{2,1,0:T(8,128)}), f32[8,8,384]{2,1,0:T(8,128)S(1)}, u32[]{:S(2)}, u32[]{:S(2)}) async-start(f32[8,8,384]{2,1,0:T(8,128)} %broadcast_in_dim.28), calls=%async_computation.7 | async-start | bytes 196608 | tf_op jit(solution)/shard_map/all_to_all | solution.py:22
Sparse Core Ops, SparseCore 0:
  10.1 68.4 all-gather.3
  90.1 66.6 all-gather.5
